TPU v7x, 512 devices: a whole 4x8x8 slice. The times are simulated.
512 devices in a mesh: gx: 32 (over z, x), gy: 16 (over y, core).
Axes of the slice: x: 4, y: 8, z: 8, core: 2. Of those that a mesh axis runs over, the one named last changes fastest.
Arguments:
- forcing: float32 [64, 256, 2048], P(None, 'gx', 'gy'), may hold values from -6 to 6
- helmholtz: float32 [64, 256, 2048], P(None, 'gx', 'gy'), may hold values from 0.1 to 4
Outputs:
- solution_field: float32 [64, 256, 2048], P(None, 'gx', 'gy')
- residual_field: float32 [64, 256, 2048], P(None, 'gx', 'gy')
All inputs are finite; a program needn't handle non-finite values.
Results may differ from a plain program's by a relative error of at most 0.000073.
Values sent between devices are 32-bit elements; how exact they have to be, the bound alone decides.
A program may use at most 64 MiB of HBM per device.

v0:
```python
import jax
import jax.numpy as jnp
from jax import lax
from jax.sharding import PartitionSpec as P

SWEEPS = 2
COARSE = 6


VERTICAL = 2.0
UPPER = 2.0
SMOOTH_LOW = 0.3
COARSE_LOW = 0.05


def extended_2(cells, sides, width):
    for axis, dim in sides:
        count = lax.axis_size(axis)
        ends = count - 1
        head = lax.slice_in_dim(cells, 0, width, axis=dim)
        tail = lax.slice_in_dim(cells, cells.shape[dim] - width, cells.shape[dim], axis=dim)
        cells = jnp.concatenate(
            [
                lax.ppermute(tail, axis, [(i, (i + 1) % count) for i in range(ends)]),
                cells,
                lax.ppermute(head, axis, [((i + 1) % count, i) for i in range(ends)]),
            ],
            axis=dim,
        )
    return cells


def passed_along(block, axis, distance):
    devices = range(lax.axis_size(axis))
    route = [(i - distance, i) for i in devices if i - distance in devices]
    return lax.ppermute(block, axis, route)


def operator(grid_field, helm_field, weight):
    pad_widths = [(0, 0)] * (grid_field.ndim - 3) + [(1, 1)] * 3
    padded = jnp.pad(grid_field, pad_widths)
    vertical_sum = padded[..., 2:, 1:-1, 1:-1] + padded[..., :-2, 1:-1, 1:-1]
    beside = (
        padded[..., 1:-1, 2:, 1:-1]
        + padded[..., 1:-1, :-2, 1:-1]
        + padded[..., 1:-1, 1:-1, 2:]
        + padded[..., 1:-1, 1:-1, :-2]
    )
    return (
        (2.0 * VERTICAL + 4.0 * weight + helm_field) * grid_field
        - VERTICAL * vertical_sum
        - weight * beside
    )


def stencil(extended, helm_field, weight):
    centre = extended[:, 1:-1, 1:-1]
    padded = jnp.pad(centre, ((1, 1), (0, 0), (0, 0)))
    vertical_sum = padded[2:] + padded[:-2]
    beside = (
        extended[:, 2:, 1:-1]
        + extended[:, :-2, 1:-1]
        + extended[:, 1:-1, 2:]
        + extended[:, 1:-1, :-2]
    )
    return (
        (2.0 * VERTICAL + 4.0 * weight + helm_field) * centre
        - VERTICAL * vertical_sum
        - weight * beside
    )


def chebyshev(iterate, target, helm_field, weight, sweeps, lower_edge, apply_fn):
    theta_mid = (UPPER + lower_edge) / 2.0
    half_width = (UPPER - lower_edge) / 2.0
    ratio = theta_mid / half_width
    inverse_diag = 1.0 / (2.0 * VERTICAL + 4.0 * weight + helm_field)
    residual_now = target - apply_fn(iterate)
    factor = 1.0 / ratio
    update = inverse_diag * residual_now / theta_mid
    for sweep_index in range(sweeps):
        iterate = iterate + update
        if sweep_index + 1 < sweeps:
            residual_now = residual_now - apply_fn(update)
            factor_new = 1.0 / (2.0 * ratio - factor)
            update = (
                factor_new * factor * update
                + 2.0 * factor_new / half_width * inverse_diag * residual_now
            )
            factor = factor_new
    return iterate


def restrict(grid_array):
    levels_z, rows_x, cols_y = grid_array.shape
    return grid_array.reshape(levels_z, rows_x // 2, 2, cols_y // 2, 2).sum(axis=(2, 4)) * 0.25


def prolong(grid_array):
    return jnp.repeat(jnp.repeat(grid_array, 2, axis=1), 2, axis=2)


def face_halo(grid_field):
    return extended_2(grid_field, (("gx", 1), ("gy", 2)), 1)


def smooth(iterate, target, helm_field, weight):

    def apply_near(grid_field):
        return stencil(face_halo(grid_field), helm_field, weight)

    return chebyshev(iterate, target, helm_field, weight, SWEEPS, SMOOTH_LOW, apply_near)


def assemble(pieces, position, concat_dim):
    result = jnp.concatenate([pieces[offset - 3] for offset in range(4)], concat_dim)
    for place in (2, 1, 0):
        candidate = jnp.concatenate([pieces[offset - place] for offset in range(4)], concat_dim)
        result = jnp.where(position == place, candidate, result)
    return result


def four_by_shifts(stacked):
    pieces = {0: stacked}
    current = stacked
    for offset in range(1, 4):
        current = passed_along(current, "gx", 1)
        pieces[-offset] = current
    current = stacked
    for offset in range(1, 4):
        current = passed_along(current, "gx", -1)
        pieces[offset] = current
    row_block = assemble(pieces, lax.axis_index("gx") % 4, 2)
    pieces = {0: row_block}
    current = row_block
    for offset in range(1, 4):
        current = passed_along(current, "gy", 1)
        pieces[-offset] = current
    current = row_block
    for offset in range(1, 4):
        current = passed_along(current, "gy", -1)
        pieces[offset] = current
    return assemble(pieces, lax.axis_index("gy") % 4, 3)


def coarse_correction(target_two, helm_two):
    stacked = jnp.stack([target_two, helm_two])
    block_data = four_by_shifts(stacked)
    target_block = block_data[0]
    helm_block = block_data[1]

    def apply_block(grid_field):
        return operator(grid_field, helm_block, 0.0625)

    solution = chebyshev(
        jnp.zeros_like(target_block),
        target_block,
        helm_block,
        0.0625,
        COARSE,
        COARSE_LOW,
        apply_block,
    )
    start_x = lax.axis_index("gx") % 4 * target_two.shape[1]
    start_y = lax.axis_index("gy") % 4 * target_two.shape[2]
    return lax.dynamic_slice(solution, (jnp.int32(0), start_x, start_y), target_two.shape)


def shards(forcing, helmholtz):
    helm_one = restrict(helmholtz)
    helm_two = restrict(helm_one)
    fine_pre = smooth(jnp.zeros_like(forcing), forcing, helmholtz, 1.0)
    target_one = restrict(forcing - stencil(face_halo(fine_pre), helmholtz, 1.0))
    one_pre = smooth(jnp.zeros_like(target_one), target_one, helm_one, 0.25)
    target_two = restrict(target_one - stencil(face_halo(one_pre), helm_one, 0.25))
    correction = coarse_correction(target_two, helm_two)
    one_post = smooth(one_pre + prolong(correction), target_one, helm_one, 0.25)
    solution_field = smooth(fine_pre + prolong(one_post), forcing, helmholtz, 1.0)
    residual_field = forcing - stencil(face_halo(solution_field), helmholtz, 1.0)
    return (solution_field, residual_field)


def solution(mesh):
    placed = (P(None, "gx", "gy"), P(None, "gx", "gy"))
    return jax.shard_map(
        shards,
        mesh=mesh,
        in_specs=placed,
        out_specs=(P(None, "gx", "gy"), P(None, "gx", "gy")),
        check_vma=False,
    )
```

profile of v0, /device:TPU:230, one launch (start us, length us, event | category | flops | bytes accessed | tf_op | source)
XLA Modules:
  0.0 283.3 jit_solution(12494327762373086273)
XLA Ops:
  0.6 5.4 %collective-permute-start.1 = (f32[64,1,128]{0,2,1:T(8,128)S(1)}, f32[64,1,128]{0,2,1:T(8,128)S(1)}, u32[]{:S(2)}, u32[]{:S(2)}) collective-permute-start(f32[64,1,128]{0,2,1:T(8,128)S(1)} %broadcast.133), channel_id=1, source_target_pairs={{0,16},{16,32},{32,48},{48,64},{64,80},{80,96},{96,112},{112,128},... | collective-permute-start | bytes 98312 | tf_op jit(solution)/shard_map/ppermute | solution.py:24
  6.1 1.9 collective-permute-start
  8.0 7.5 %collective-permute-done = f32[64,1,128]{0,2,1:T(8,128)S(1)} collective-permute-done((f32[64,1,128]{0,2,1:T(8,128)S(1)}, f32[64,1,128]{0,2,1:T(8,128)S(1)}, u32[]{:S(2)}, u32[]{:S(2)}) %collective-permute-start) | collective-permute-done | bytes 32800 | tf_op jit(solution)/shard_map/ppermute | solution.py:26
  15.6 2.1 collective-permute-start.2
  17.7 2.5 collective-permute-start.3
  20.7 3.3 %collective-permute-done.3 = f32[64,10,1]{0,2,1:T(1,128)S(1)} collective-permute-done((f32[64,10,1]{0,2,1:T(1,128)S(1)}, f32[64,10,1]{0,2,1:T(1,128)S(1)}, u32[]{:S(2)}, u32[]{:S(2)}) %collective-permute-start.3) | collective-permute-done | bytes 2592 | tf_op jit(solution)/shard_map/ppermute | solution.py:24
  24.4 1.9 collective-permute-start.5
  26.3 3.9 %collective-permute-start.4 = (f32[64,1,128]{0,2,1:T(8,128)S(1)}, f32[64,1,128]{0,2,1:T(8,128)S(1)}, u32[]{:S(2)}, u32[]{:S(2)}) collective-permute-start(f32[64,1,128]{0,2,1:T(8,128)S(1)} %get-tuple-element.45), channel_id=1, source_target_pairs={{16,0},{32,16},{48,32},{64,48},{80,64},{96,80},{112,96},{128,112},... | collective-permute-start | bytes 98312 | tf_op jit(solution)/shard_map/ppermute | solution.py:26
  30.5 5.2 %collective-permute-done.4 = f32[64,1,128]{0,2,1:T(8,128)S(1)} collective-permute-done((f32[64,1,128]{0,2,1:T(8,128)S(1)}, f32[64,1,128]{0,2,1:T(8,128)S(1)}, u32[]{:S(2)}, u32[]{:S(2)}) %collective-permute-start.4) | collective-permute-done | bytes 32800 | tf_op jit(solution)/shard_map/ppermute | solution.py:26
  35.8 1.9 collective-permute-start.6
  37.7 2.4 collective-permute-start.7
  40.2 3.7 %collective-permute-done.7 = f32[64,10,1]{0,2,1:T(1,128)S(1)} collective-permute-done((f32[64,10,1]{0,2,1:T(1,128)S(1)}, f32[64,10,1]{0,2,1:T(1,128)S(1)}, u32[]{:S(2)}, u32[]{:S(2)}) %collective-permute-start.7) | collective-permute-done | bytes 2592 | tf_op jit(solution)/shard_map/ppermute | solution.py:24
  44.4 1.9 collective-permute-start.9
  46.3 3.9 %collective-permute-start.8 = (f32[64,1,128]{0,2,1:T(8,128)S(1)}, f32[64,1,128]{0,2,1:T(8,128)S(1)}, u32[]{:S(2)}, u32[]{:S(2)}) collective-permute-start(f32[64,1,128]{0,2,1:T(8,128)S(1)} %get-tuple-element.43), channel_id=1, source_target_pairs={{16,0},{32,16},{48,32},{64,48},{80,64},{96,80},{112,96},{128,112},... | collective-permute-start | bytes 98312 | tf_op jit(solution)/shard_map/ppermute | solution.py:26
  50.3 5.2 %collective-permute-start.13 = (f32[64,1,64]{0,2,1:T(8,128)S(1)}, f32[64,1,64]{0,2,1:T(8,128)S(1)}, u32[]{:S(2)}, u32[]{:S(2)}) collective-permute-start(f32[64,1,64]{0,2,1:T(8,128)S(1)} %broadcast.140), channel_id=1, source_target_pairs={{0,16},{16,32},{32,48},{48,64},{64,80},{80,96},{96,112},{112,128},... | collective-permute-start | bytes 49160 | tf_op jit(solution)/shard_map/ppermute | solution.py:24
  57.9 1.9 collective-permute-start.10
  59.9 2.4 collective-permute-start.11
  62.3 2.4 collective-permute-done.12
  64.7 2.0 collective-permute-start.14
  66.7 2.3 collective-permute-start.15
  69.9 2.9 %collective-permute-done.15 = f32[64,6,1]{0,2,1:T(1,128)S(1)} collective-permute-done((f32[64,6,1]{0,2,1:T(1,128)S(1)}, f32[64,6,1]{0,2,1:T(1,128)S(1)}, u32[]{:S(2)}, u32[]{:S(2)}) %collective-permute-start.15) | collective-permute-done | bytes 1568 | tf_op jit(solution)/shard_map/ppermute | solution.py:24
  73.0 7.2 %collective-permute-start.17 = (f32[64,1,64]{0,2,1:T(8,128)S(1)}, f32[64,1,64]{0,2,1:T(8,128)S(1)}, u32[]{:S(2)}, u32[]{:S(2)}) collective-permute-start(f32[64,1,64]{0,2,1:T(8,128)S(1)} %get-tuple-element.64), channel_id=1, source_target_pairs={{0,16},{16,32},{32,48},{48,64},{64,80},{80,96},{96,112},{112,128},... | collective-permute-start | bytes 49160 | tf_op jit(solution)/shard_map/ppermute | solution.py:24
  82.2 7.2 %collective-permute-done.16 = f32[64,1,64]{0,2,1:T(8,128)S(1)} collective-permute-done((f32[64,1,64]{0,2,1:T(8,128)S(1)}, f32[64,1,64]{0,2,1:T(8,128)S(1)}, u32[]{:S(2)}, u32[]{:S(2)}) %collective-permute-start.16) | collective-permute-done | bytes 16416 | tf_op jit(solution)/shard_map/ppermute | solution.py:26
  91.3 2.4 collective-permute-start.19
  93.7 3.7 %collective-permute-done.19 = f32[64,6,1]{0,2,1:T(1,128)S(1)} collective-permute-done((f32[64,6,1]{0,2,1:T(1,128)S(1)}, f32[64,6,1]{0,2,1:T(1,128)S(1)}, u32[]{:S(2)}, u32[]{:S(2)}) %collective-permute-start.19) | collective-permute-done | bytes 1568 | tf_op jit(solution)/shard_map/ppermute | solution.py:24
  97.6 1.9 collective-permute-start.21
  99.5 3.9 %collective-permute-start.20 = (f32[64,1,64]{0,2,1:T(8,128)S(1)}, f32[64,1,64]{0,2,1:T(8,128)S(1)}, u32[]{:S(2)}, u32[]{:S(2)}) collective-permute-start(f32[64,1,64]{0,2,1:T(8,128)S(1)} %get-tuple-element.63), channel_id=1, source_target_pairs={{16,0},{32,16},{48,32},{64,48},{80,64},{96,80},{112,96},{128,112},... | collective-permute-start | bytes 49160 | tf_op jit(solution)/shard_map/ppermute | solution.py:26
  103.5 5.2 %collective-permute-done.20 = f32[64,1,64]{0,2,1:T(8,128)S(1)} collective-permute-done((f32[64,1,64]{0,2,1:T(8,128)S(1)}, f32[64,1,64]{0,2,1:T(8,128)S(1)}, u32[]{:S(2)}, u32[]{:S(2)}) %collective-permute-start.20) | collective-permute-done | bytes 16416 | tf_op jit(solution)/shard_map/ppermute | solution.py:26
  110.6 2.4 collective-permute-start.23
  113.0 3.7 %collective-permute-done.23 = f32[64,6,1]{0,2,1:T(1,128)S(1)} collective-permute-done((f32[64,6,1]{0,2,1:T(1,128)S(1)}, f32[64,6,1]{0,2,1:T(1,128)S(1)}, u32[]{:S(2)}, u32[]{:S(2)}) %collective-permute-start.23) | collective-permute-done | bytes 1568 | tf_op jit(solution)/shard_map/ppermute | solution.py:24
  117.1 1.9 collective-permute-start.27
  119.1 3.9 %collective-permute-start.24 = (f32[2,64,2,32]{1,3,2,0:T(8,128)S(1)}, f32[2,64,2,32]{1,3,2,0:T(8,128)S(1)}, u32[]{:S(2)}, u32[]{:S(2)}) collective-permute-start(f32[2,64,2,32]{1,3,2,0:T(8,128)S(1)} %pad_maximum_fusion.84), channel_id=1, source_target_pairs={{16,0},{32,16},{48,32},{64,48},{80,64},{96,80},{112,96},{128,112},... | collective-permute-start | bytes 98312 | tf_op jit(solution)/shard_map/ppermute | solution.py:36
  123.3 5.2 %collective-permute-start.28 = (f32[2,64,2,32]{1,3,2,0:T(8,128)S(1)}, f32[2,64,2,32]{1,3,2,0:T(8,128)S(1)}, u32[]{:S(2)}, u32[]{:S(2)}) collective-permute-start(f32[2,64,2,32]{1,3,2,0:T(8,128)S(1)} %collective-permute-done.27), channel_id=1, source_target_pairs={{0,16},{16,32},{32,48},{48,64},{64,80},{80,96},{96,112},{112,128},... | collective-permute-start | bytes 98312 | tf_op jit(solution)/shard_map/ppermute | solution.py:36
  130.5 7.5 %collective-permute-start.29 = (f32[2,64,2,32]{1,3,2,0:T(8,128)S(1)}, f32[2,64,2,32]{1,3,2,0:T(8,128)S(1)}, u32[]{:S(2)}, u32[]{:S(2)}) collective-permute-start(f32[2,64,2,32]{1,3,2,0:T(8,128)S(1)} %collective-permute-done.28), channel_id=1, source_target_pairs={{0,16},{16,32},{32,48},{48,64},{64,80},{80,96},{96,112},{112,128},... | collective-permute-start | bytes 98312 | tf_op jit(solution)/shard_map/ppermute | solution.py:36
  140.0 7.5 %collective-permute-done.26 = f32[2,64,2,32]{1,3,2,0:T(8,128)S(1)} collective-permute-done((f32[2,64,2,32]{1,3,2,0:T(8,128)S(1)}, f32[2,64,2,32]{1,3,2,0:T(8,128)S(1)}, u32[]{:S(2)}, u32[]{:S(2)}) %collective-permute-start.26) | collective-permute-done | bytes 32800 | tf_op jit(solution)/shard_map/ppermute | solution.py:36
  149.5 4.9 %collective-permute-start.30 = (f32[2,64,8,32]{1,3,2,0:T(8,128)S(1)}, f32[2,64,8,32]{1,3,2,0:T(8,128)S(1)}, u32[]{:S(2)}, u32[]{:S(2)}) collective-permute-start(f32[2,64,8,32]{1,3,2,0:T(8,128)S(1)} %maximum_select_fusion.3), channel_id=1, source_target_pairs={{1,0},{2,1},{3,2},{4,3},{5,4},{6,5},{7,6},{8,7},{9,8},{10,9},{11,1... | collective-permute-start | bytes 393224 | tf_op jit(solution)/shard_map/ppermute | solution.py:36
  154.3 2.1 collective-permute-done.33
  158.4 4.9 %collective-permute-start.31 = (f32[2,64,8,32]{1,3,2,0:T(8,128)S(1)}, f32[2,64,8,32]{1,3,2,0:T(8,128)}, u32[]{:S(2)}, u32[]{:S(2)}) collective-permute-start(f32[2,64,8,32]{1,3,2,0:T(8,128)S(1)} %collective-permute-done.30), channel_id=1, source_target_pairs={{1,0},{2,1},{3,2},{4,3},{5,4},{6,5},{7,6},{8,7},{9,8},{10,9},{11,1... | collective-permute-start | bytes 393224 | tf_op jit(solution)/shard_map/ppermute | solution.py:36
  163.2 2.2 collective-permute-done.34
  167.4 4.9 %collective-permute-start.32 = (f32[2,64,8,32]{1,3,2,0:T(8,128)}, f32[2,64,8,32]{1,3,2,0:T(8,128)}, u32[]{:S(2)}, u32[]{:S(2)}) collective-permute-start(f32[2,64,8,32]{1,3,2,0:T(8,128)} %collective-permute-done.31), channel_id=1, source_target_pairs={{1,0},{2,1},{3,2},{4,3},{5,4},{6,5},{7,6},{8,7},{9,8},{10,9},{11,1... | collective-permute-start | bytes 393224 | tf_op jit(solution)/shard_map/ppermute | solution.py:36
  172.3 2.4 collective-permute-done.35
  183.5 3.9 %collective-permute-start.36 = (f32[64,1,64]{0,2,1:T(8,128)S(1)}, f32[64,1,64]{0,2,1:T(8,128)S(1)}, u32[]{:S(2)}, u32[]{:S(2)}) collective-permute-start(f32[64,1,64]{0,2,1:T(8,128)S(1)} %get-tuple-element.59), channel_id=1, source_target_pairs={{16,0},{32,16},{48,32},{64,48},{80,64},{96,80},{112,96},{128,112},... | collective-permute-start | bytes 49160 | tf_op jit(solution)/shard_map/ppermute | solution.py:26
  187.5 5.2 %collective-permute-done.36 = f32[64,1,64]{0,2,1:T(8,128)S(1)} collective-permute-done((f32[64,1,64]{0,2,1:T(8,128)S(1)}, f32[64,1,64]{0,2,1:T(8,128)S(1)}, u32[]{:S(2)}, u32[]{:S(2)}) %collective-permute-start.36) | collective-permute-done | bytes 16416 | tf_op jit(solution)/shard_map/ppermute | solution.py:26
  192.7 3.9 %collective-permute-start.38 = (f32[64,6,1]{0,2,1:T(1,128)S(1)}, f32[64,6,1]{0,2,1:T(1,128)S(1)}, u32[]{:S(2)}, u32[]{:S(2)}) collective-permute-start(f32[64,6,1]{0,2,1:T(1,128)S(1)} %get-tuple-element.48), channel_id=1, source_target_pairs={{1,0},{2,1},{3,2},{4,3},{5,4},{6,5},{7,6},{8,7},{9,8},{10,9},{11,1... | collective-permute-start | bytes 4616 | tf_op jit(solution)/shard_map/ppermute | solution.py:26
  198.5 4.2 %collective-permute-done.39 = f32[64,6,1]{0,2,1:T(1,128)S(1)} collective-permute-done((f32[64,6,1]{0,2,1:T(1,128)S(1)}, f32[64,6,1]{0,2,1:T(1,128)S(1)}, u32[]{:S(2)}, u32[]{:S(2)}) %collective-permute-start.39) | collective-permute-done | bytes 1568 | tf_op jit(solution)/shard_map/ppermute | solution.py:24
  204.8 3.9 %collective-permute-start.40 = (f32[64,1,64]{0,2,1:T(8,128)S(1)}, f32[64,1,64]{0,2,1:T(8,128)S(1)}, u32[]{:S(2)}, u32[]{:S(2)}) collective-permute-start(f32[64,1,64]{0,2,1:T(8,128)S(1)} %get-tuple-element.57), channel_id=1, source_target_pairs={{16,0},{32,16},{48,32},{64,48},{80,64},{96,80},{112,96},{128,112},... | collective-permute-start | bytes 49160 | tf_op jit(solution)/shard_map/ppermute | solution.py:26
  208.7 5.2 %collective-permute-done.40 = f32[64,1,64]{0,2,1:T(8,128)S(1)} collective-permute-done((f32[64,1,64]{0,2,1:T(8,128)S(1)}, f32[64,1,64]{0,2,1:T(8,128)S(1)}, u32[]{:S(2)}, u32[]{:S(2)}) %collective-permute-start.40) | collective-permute-done | bytes 16416 | tf_op jit(solution)/shard_map/ppermute | solution.py:26
  215.8 2.4 collective-permute-start.43
  218.3 3.7 %collective-permute-done.43 = f32[64,6,1]{0,2,1:T(1,128)S(1)} collective-permute-done((f32[64,6,1]{0,2,1:T(1,128)S(1)}, f32[64,6,1]{0,2,1:T(1,128)S(1)}, u32[]{:S(2)}, u32[]{:S(2)}) %collective-permute-start.43) | collective-permute-done | bytes 1568 | tf_op jit(solution)/shard_map/ppermute | solution.py:24
  222.5 1.9 collective-permute-start.45
  224.4 3.9 %collective-permute-start.44 = (f32[64,1,128]{0,2,1:T(8,128)S(1)}, f32[64,1,128]{0,2,1:T(8,128)S(1)}, u32[]{:S(2)}, u32[]{:S(2)}) collective-permute-start(f32[64,1,128]{0,2,1:T(8,128)S(1)} %get-tuple-element.39), channel_id=1, source_target_pairs={{16,0},{32,16},{48,32},{64,48},{80,64},{96,80},{112,96},{128,112},... | collective-permute-start | bytes 98312 | tf_op jit(solution)/shard_map/ppermute | solution.py:26
  228.7 5.2 %collective-permute-done.44 = f32[64,1,128]{0,2,1:T(8,128)S(1)} collective-permute-done((f32[64,1,128]{0,2,1:T(8,128)S(1)}, f32[64,1,128]{0,2,1:T(8,128)S(1)}, u32[]{:S(2)}, u32[]{:S(2)}) %collective-permute-start.44) | collective-permute-done | bytes 32800 | tf_op jit(solution)/shard_map/ppermute | solution.py:26
  235.9 2.4 collective-permute-start.47
  238.3 3.7 %collective-permute-done.47 = f32[64,10,1]{0,2,1:T(1,128)S(1)} collective-permute-done((f32[64,10,1]{0,2,1:T(1,128)S(1)}, f32[64,10,1]{0,2,1:T(1,128)S(1)}, u32[]{:S(2)}, u32[]{:S(2)}) %collective-permute-start.47) | collective-permute-done | bytes 2592 | tf_op jit(solution)/shard_map/ppermute | solution.py:24
  242.5 1.9 collective-permute-start.49
  244.4 3.9 %collective-permute-start.48 = (f32[64,1,128]{0,2,1:T(8,128)S(1)}, f32[64,1,128]{0,2,1:T(8,128)S(1)}, u32[]{:S(2)}, u32[]{:S(2)}) collective-permute-start(f32[64,1,128]{0,2,1:T(8,128)S(1)} %get-tuple-element.37), channel_id=1, source_target_pairs={{16,0},{32,16},{48,32},{64,48},{80,64},{96,80},{112,96},{128,112},... | collective-permute-start | bytes 98312 | tf_op jit(solution)/shard_map/ppermute | solution.py:26
  248.6 5.2 %collective-permute-done.48 = f32[64,1,128]{0,2,1:T(8,128)S(1)} collective-permute-done((f32[64,1,128]{0,2,1:T(8,128)S(1)}, f32[64,1,128]{0,2,1:T(8,128)S(1)}, u32[]{:S(2)}, u32[]{:S(2)}) %collective-permute-start.48) | collective-permute-done | bytes 32800 | tf_op jit(solution)/shard_map/ppermute | solution.py:26
  255.8 2.4 collective-permute-start.51
  258.2 3.7 %collective-permute-done.51 = f32[64,10,1]{0,2,1:T(1,128)S(1)} collective-permute-done((f32[64,10,1]{0,2,1:T(1,128)S(1)}, f32[64,10,1]{0,2,1:T(1,128)S(1)}, u32[]{:S(2)}, u32[]{:S(2)}) %collective-permute-start.51) | collective-permute-done | bytes 2592 | tf_op jit(solution)/shard_map/ppermute | solution.py:24
  262.5 1.9 collective-permute-start.53
  264.4 3.9 %collective-permute-start.52 = (f32[64,1,128]{0,2,1:T(8,128)S(1)}, f32[64,1,128]{0,2,1:T(8,128)S(1)}, u32[]{:S(2)}, u32[]{:S(2)}) collective-permute-start(f32[64,1,128]{0,2,1:T(8,128)S(1)} %get-tuple-element.35), channel_id=1, source_target_pairs={{16,0},{32,16},{48,32},{64,48},{80,64},{96,80},{112,96},{128,112},... | collective-permute-start | bytes 98312 | tf_op jit(solution)/shard_map/ppermute | solution.py:26
  268.7 5.2 %collective-permute-done.52 = f32[64,1,128]{0,2,1:T(8,128)S(1)} collective-permute-done((f32[64,1,128]{0,2,1:T(8,128)S(1)}, f32[64,1,128]{0,2,1:T(8,128)S(1)}, u32[]{:S(2)}, u32[]{:S(2)}) %collective-permute-start.52) | collective-permute-done | bytes 32800 | tf_op jit(solution)/shard_map/ppermute | solution.py:26
  275.8 2.4 collective-permute-start.55
  279.2 2.8 %collective-permute-done.55 = f32[64,10,1]{0,2,1:T(1,128)S(1)} collective-permute-done((f32[64,10,1]{0,2,1:T(1,128)S(1)}, f32[64,10,1]{0,2,1:T(1,128)S(1)}, u32[]{:S(2)}, u32[]{:S(2)}) %collective-permute-start.55) | collective-permute-done | bytes 2592 | tf_op jit(solution)/shard_map/ppermute | solution.py:24
  (113 shorter events, 46.5 us)
Async XLA Ops:
  0.6 7.3 %collective-permute-start.1 = (f32[64,1,128]{0,2,1:T(8,128)S(1)}, f32[64,1,128]{0,2,1:T(8,128)S(1)}, u32[]{:S(2)}, u32[]{:S(2)}) collective-permute-start(f32[64,1,128]{0,2,1:T(8,128)S(1)} %broadcast.133), channel_id=1, source_target_pairs={{0,16},{16,32},{32,48},{48,64},{64,80},{80,96},{96,112},{112,128},... | collective-permute-start | bytes 98312 | tf_op jit(solution)/shard_map/ppermute | solution.py:24
  6.1 9.5 %collective-permute-start = (f32[64,1,128]{0,2,1:T(8,128)S(1)}, f32[64,1,128]{0,2,1:T(8,128)S(1)}, u32[]{:S(2)}, u32[]{:S(2)}) collective-permute-start(f32[64,1,128]{0,2,1:T(8,128)S(1)} %broadcast.133), channel_id=1, source_target_pairs={{16,0},{32,16},{48,32},{64,48},{80,64},{96,80},{112,96},{128,112},... | collective-permute-start | bytes 98312 | tf_op jit(solution)/shard_map/ppermute | solution.py:26
  15.6 4.7 %copy-start = (f32[64,8,128]{2,1,0:T(8,128)S(1)}, f32[64,8,128]{2,1,0:T(8,128)}, u32[]{:S(2)}) copy-start(f32[64,8,128]{2,1,0:T(8,128)} %param.3) | copy-start | bytes 786436
  15.6 5.1 %collective-permute-start.2 = (f32[64,10,1]{0,2,1:T(1,128)S(1)}, f32[64,10,1]{0,2,1:T(1,128)S(1)}, u32[]{:S(2)}, u32[]{:S(2)}) collective-permute-start(f32[64,10,1]{0,2,1:T(1,128)S(1)} %get-tuple-element.32), channel_id=1, source_target_pairs={{1,0},{2,1},{3,2},{4,3},{5,4},{6,5},{7,6},{8,7},{9,8},{10,9},{11,1... | collective-permute-start | bytes 7688 | tf_op jit(solution)/shard_map/ppermute | solution.py:26
  17.7 2.8 copy-start.1
  17.7 6.3 %collective-permute-start.3 = (f32[64,10,1]{0,2,1:T(1,128)S(1)}, f32[64,10,1]{0,2,1:T(1,128)S(1)}, u32[]{:S(2)}, u32[]{:S(2)}) collective-permute-start(f32[64,10,1]{0,2,1:T(1,128)S(1)} %get-tuple-element.33), channel_id=1, source_target_pairs={{0,1},{1,2},{2,3},{3,4},{4,5},{5,6},{6,7},{7,8},{8,9},{9,10},{10,1... | collective-permute-start | bytes 7688 | tf_op jit(solution)/shard_map/ppermute | solution.py:24
  24.4 6.2 %collective-permute-start.5 = (f32[64,1,128]{0,2,1:T(8,128)S(1)}, f32[64,1,128]{0,2,1:T(8,128)S(1)}, u32[]{:S(2)}, u32[]{:S(2)}) collective-permute-start(f32[64,1,128]{0,2,1:T(8,128)S(1)} %get-tuple-element.44), channel_id=1, source_target_pairs={{0,16},{16,32},{32,48},{48,64},{64,80},{80,96},{96,112},{112,128},... | collective-permute-start | bytes 98312 | tf_op jit(solution)/shard_map/ppermute | solution.py:24
  26.3 9.5 %collective-permute-start.4 = (f32[64,1,128]{0,2,1:T(8,128)S(1)}, f32[64,1,128]{0,2,1:T(8,128)S(1)}, u32[]{:S(2)}, u32[]{:S(2)}) collective-permute-start(f32[64,1,128]{0,2,1:T(8,128)S(1)} %get-tuple-element.45), channel_id=1, source_target_pairs={{16,0},{32,16},{48,32},{64,48},{80,64},{96,80},{112,96},{128,112},... | collective-permute-start | bytes 98312 | tf_op jit(solution)/shard_map/ppermute | solution.py:26
  35.8 4.3 %collective-permute-start.6 = (f32[64,10,1]{0,2,1:T(1,128)S(1)}, f32[64,10,1]{0,2,1:T(1,128)S(1)}, u32[]{:S(2)}, u32[]{:S(2)}) collective-permute-start(f32[64,10,1]{0,2,1:T(1,128)S(1)} %get-tuple-element.30), channel_id=1, source_target_pairs={{1,0},{2,1},{3,2},{4,3},{5,4},{6,5},{7,6},{8,7},{9,8},{10,9},{11,1... | collective-permute-start | bytes 7688 | tf_op jit(solution)/shard_map/ppermute | solution.py:26
  37.7 6.1 %collective-permute-start.7 = (f32[64,10,1]{0,2,1:T(1,128)S(1)}, f32[64,10,1]{0,2,1:T(1,128)S(1)}, u32[]{:S(2)}, u32[]{:S(2)}) collective-permute-start(f32[64,10,1]{0,2,1:T(1,128)S(1)} %get-tuple-element.31), channel_id=1, source_target_pairs={{0,1},{1,2},{2,3},{3,4},{4,5},{5,6},{6,7},{7,8},{8,9},{9,10},{10,1... | collective-permute-start | bytes 7688 | tf_op jit(solution)/shard_map/ppermute | solution.py:24
  44.4 13.5 %collective-permute-start.9 = (f32[64,1,128]{0,2,1:T(8,128)S(1)}, f32[64,1,128]{0,2,1:T(8,128)S(1)}, u32[]{:S(2)}, u32[]{:S(2)}) collective-permute-start(f32[64,1,128]{0,2,1:T(8,128)S(1)} %get-tuple-element.42), channel_id=1, source_target_pairs={{0,16},{16,32},{32,48},{48,64},{64,80},{80,96},{96,112},{112,128},... | collective-permute-start | bytes 98312 | tf_op jit(solution)/shard_map/ppermute | solution.py:24
  46.3 11.6 %collective-permute-start.8 = (f32[64,1,128]{0,2,1:T(8,128)S(1)}, f32[64,1,128]{0,2,1:T(8,128)S(1)}, u32[]{:S(2)}, u32[]{:S(2)}) collective-permute-start(f32[64,1,128]{0,2,1:T(8,128)S(1)} %get-tuple-element.43), channel_id=1, source_target_pairs={{16,0},{32,16},{48,32},{64,48},{80,64},{96,80},{112,96},{128,112},... | collective-permute-start | bytes 98312 | tf_op jit(solution)/shard_map/ppermute | solution.py:26
  50.3 12.0 %collective-permute-start.13 = (f32[64,1,64]{0,2,1:T(8,128)S(1)}, f32[64,1,64]{0,2,1:T(8,128)S(1)}, u32[]{:S(2)}, u32[]{:S(2)}) collective-permute-start(f32[64,1,64]{0,2,1:T(8,128)S(1)} %broadcast.140), channel_id=1, source_target_pairs={{0,16},{16,32},{32,48},{48,64},{64,80},{80,96},{96,112},{112,128},... | collective-permute-start | bytes 49160 | tf_op jit(solution)/shard_map/ppermute | solution.py:24
  55.5 9.1 %collective-permute-start.12 = (f32[64,1,64]{0,2,1:T(8,128)S(1)}, f32[64,1,64]{0,2,1:T(8,128)S(1)}, u32[]{:S(2)}, u32[]{:S(2)}) collective-permute-start(f32[64,1,64]{0,2,1:T(8,128)S(1)} %broadcast.140), channel_id=1, source_target_pairs={{16,0},{32,16},{48,32},{64,48},{80,64},{96,80},{112,96},{128,112},... | collective-permute-start | bytes 49160 | tf_op jit(solution)/shard_map/ppermute | solution.py:26
  57.9 11.1 %collective-permute-start.10 = (f32[64,10,1]{0,2,1:T(1,128)S(1)}, f32[64,10,1]{0,2,1:T(1,128)S(1)}, u32[]{:S(2)}, u32[]{:S(2)}) collective-permute-start(f32[64,10,1]{0,2,1:T(1,128)S(1)} %get-tuple-element.28), channel_id=1, source_target_pairs={{1,0},{2,1},{3,2},{4,3},{5,4},{6,5},{7,6},{8,7},{9,8},{10,9},{11,1... | collective-permute-start | bytes 7688 | tf_op jit(solution)/shard_map/ppermute | solution.py:26
  59.9 9.2 %collective-permute-start.11 = (f32[64,10,1]{0,2,1:T(1,128)S(1)}, f32[64,10,1]{0,2,1:T(1,128)S(1)}, u32[]{:S(2)}, u32[]{:S(2)}) collective-permute-start(f32[64,10,1]{0,2,1:T(1,128)S(1)} %get-tuple-element.29), channel_id=1, source_target_pairs={{0,1},{1,2},{2,3},{3,4},{4,5},{5,6},{6,7},{7,8},{8,9},{9,10},{10,1... | collective-permute-start | bytes 7688 | tf_op jit(solution)/shard_map/ppermute | solution.py:24
  64.7 5.2 %collective-permute-start.14 = (f32[64,6,1]{0,2,1:T(1,128)S(1)}, f32[64,6,1]{0,2,1:T(1,128)S(1)}, u32[]{:S(2)}, u32[]{:S(2)}) collective-permute-start(f32[64,6,1]{0,2,1:T(1,128)S(1)} %get-tuple-element.54), channel_id=1, source_target_pairs={{1,0},{2,1},{3,2},{4,3},{5,4},{6,5},{7,6},{8,7},{9,8},{10,9},{11,1... | collective-permute-start | bytes 4616 | tf_op jit(solution)/shard_map/ppermute | solution.py:26
  66.7 6.1 %collective-permute-start.15 = (f32[64,6,1]{0,2,1:T(1,128)S(1)}, f32[64,6,1]{0,2,1:T(1,128)S(1)}, u32[]{:S(2)}, u32[]{:S(2)}) collective-permute-start(f32[64,6,1]{0,2,1:T(1,128)S(1)} %get-tuple-element.55), channel_id=1, source_target_pairs={{0,1},{1,2},{2,3},{3,4},{4,5},{5,6},{6,7},{7,8},{8,9},{9,10},{10,1... | collective-permute-start | bytes 4616 | tf_op jit(solution)/shard_map/ppermute | solution.py:24
  73.0 9.2 %collective-permute-start.17 = (f32[64,1,64]{0,2,1:T(8,128)S(1)}, f32[64,1,64]{0,2,1:T(8,128)S(1)}, u32[]{:S(2)}, u32[]{:S(2)}) collective-permute-start(f32[64,1,64]{0,2,1:T(8,128)S(1)} %get-tuple-element.64), channel_id=1, source_target_pairs={{0,16},{16,32},{32,48},{48,64},{64,80},{80,96},{96,112},{112,128},... | collective-permute-start | bytes 49160 | tf_op jit(solution)/shard_map/ppermute | solution.py:24
  80.2 9.1 %collective-permute-start.16 = (f32[64,1,64]{0,2,1:T(8,128)S(1)}, f32[64,1,64]{0,2,1:T(8,128)S(1)}, u32[]{:S(2)}, u32[]{:S(2)}) collective-permute-start(f32[64,1,64]{0,2,1:T(8,128)S(1)} %get-tuple-element.65), channel_id=1, source_target_pairs={{16,0},{32,16},{48,32},{64,48},{80,64},{96,80},{112,96},{128,112},... | collective-permute-start | bytes 49160 | tf_op jit(solution)/shard_map/ppermute | solution.py:26
  89.4 4.3 %collective-permute-start.18 = (f32[64,6,1]{0,2,1:T(1,128)S(1)}, f32[64,6,1]{0,2,1:T(1,128)S(1)}, u32[]{:S(2)}, u32[]{:S(2)}) collective-permute-start(f32[64,6,1]{0,2,1:T(1,128)S(1)} %get-tuple-element.52), channel_id=1, source_target_pairs={{1,0},{2,1},{3,2},{4,3},{5,4},{6,5},{7,6},{8,7},{9,8},{10,9},{11,1... | collective-permute-start | bytes 4616 | tf_op jit(solution)/shard_map/ppermute | solution.py:26
  91.3 6.1 %collective-permute-start.19 = (f32[64,6,1]{0,2,1:T(1,128)S(1)}, f32[64,6,1]{0,2,1:T(1,128)S(1)}, u32[]{:S(2)}, u32[]{:S(2)}) collective-permute-start(f32[64,6,1]{0,2,1:T(1,128)S(1)} %get-tuple-element.53), channel_id=1, source_target_pairs={{0,1},{1,2},{2,3},{3,4},{4,5},{5,6},{6,7},{7,8},{8,9},{9,10},{10,1... | collective-permute-start | bytes 4616 | tf_op jit(solution)/shard_map/ppermute | solution.py:24
  97.6 5.9 %collective-permute-start.21 = (f32[64,1,64]{0,2,1:T(8,128)S(1)}, f32[64,1,64]{0,2,1:T(8,128)S(1)}, u32[]{:S(2)}, u32[]{:S(2)}) collective-permute-start(f32[64,1,64]{0,2,1:T(8,128)S(1)} %get-tuple-element.62), channel_id=1, source_target_pairs={{0,16},{16,32},{32,48},{48,64},{64,80},{80,96},{96,112},{112,128},... | collective-permute-start | bytes 49160 | tf_op jit(solution)/shard_map/ppermute | solution.py:24
  99.5 9.1 %collective-permute-start.20 = (f32[64,1,64]{0,2,1:T(8,128)S(1)}, f32[64,1,64]{0,2,1:T(8,128)S(1)}, u32[]{:S(2)}, u32[]{:S(2)}) collective-permute-start(f32[64,1,64]{0,2,1:T(8,128)S(1)} %get-tuple-element.63), channel_id=1, source_target_pairs={{16,0},{32,16},{48,32},{64,48},{80,64},{96,80},{112,96},{128,112},... | collective-permute-start | bytes 49160 | tf_op jit(solution)/shard_map/ppermute | solution.py:26
  108.7 4.3 %collective-permute-start.22 = (f32[64,6,1]{0,2,1:T(1,128)S(1)}, f32[64,6,1]{0,2,1:T(1,128)S(1)}, u32[]{:S(2)}, u32[]{:S(2)}) collective-permute-start(f32[64,6,1]{0,2,1:T(1,128)S(1)} %get-tuple-element.50), channel_id=1, source_target_pairs={{1,0},{2,1},{3,2},{4,3},{5,4},{6,5},{7,6},{8,7},{9,8},{10,9},{11,1... | collective-permute-start | bytes 4616 | tf_op jit(solution)/shard_map/ppermute | solution.py:26
  110.6 6.1 %collective-permute-start.23 = (f32[64,6,1]{0,2,1:T(1,128)S(1)}, f32[64,6,1]{0,2,1:T(1,128)S(1)}, u32[]{:S(2)}, u32[]{:S(2)}) collective-permute-start(f32[64,6,1]{0,2,1:T(1,128)S(1)} %get-tuple-element.51), channel_id=1, source_target_pairs={{0,1},{1,2},{2,3},{3,4},{4,5},{5,6},{6,7},{7,8},{8,9},{9,10},{10,1... | collective-permute-start | bytes 4616 | tf_op jit(solution)/shard_map/ppermute | solution.py:24
  117.1 6.2 %collective-permute-start.27 = (f32[2,64,2,32]{1,3,2,0:T(8,128)S(1)}, f32[2,64,2,32]{1,3,2,0:T(8,128)S(1)}, u32[]{:S(2)}, u32[]{:S(2)}) collective-permute-start(f32[2,64,2,32]{1,3,2,0:T(8,128)S(1)} %pad_maximum_fusion.84), channel_id=1, source_target_pairs={{0,16},{16,32},{32,48},{48,64},{64,80},{80,96},{96,112},{112,128},... | collective-permute-start | bytes 98312 | tf_op jit(solution)/shard_map/ppermute | solution.py:36
  119.1 9.5 %collective-permute-start.24 = (f32[2,64,2,32]{1,3,2,0:T(8,128)S(1)}, f32[2,64,2,32]{1,3,2,0:T(8,128)S(1)}, u32[]{:S(2)}, u32[]{:S(2)}) collective-permute-start(f32[2,64,2,32]{1,3,2,0:T(8,128)S(1)} %pad_maximum_fusion.84), channel_id=1, source_target_pairs={{16,0},{32,16},{48,32},{64,48},{80,64},{96,80},{112,96},{128,112},... | collective-permute-start | bytes 98312 | tf_op jit(solution)/shard_map/ppermute | solution.py:36
  123.3 7.2 %collective-permute-start.28 = (f32[2,64,2,32]{1,3,2,0:T(8,128)S(1)}, f32[2,64,2,32]{1,3,2,0:T(8,128)S(1)}, u32[]{:S(2)}, u32[]{:S(2)}) collective-permute-start(f32[2,64,2,32]{1,3,2,0:T(8,128)S(1)} %collective-permute-done.27), channel_id=1, source_target_pairs={{0,16},{16,32},{32,48},{48,64},{64,80},{80,96},{96,112},{112,128},... | collective-permute-start | bytes 98312 | tf_op jit(solution)/shard_map/ppermute | solution.py:36
  128.5 9.5 %collective-permute-start.25 = (f32[2,64,2,32]{1,3,2,0:T(8,128)S(1)}, f32[2,64,2,32]{1,3,2,0:T(8,128)S(1)}, u32[]{:S(2)}, u32[]{:S(2)}) collective-permute-start(f32[2,64,2,32]{1,3,2,0:T(8,128)S(1)} %collective-permute-done.24), channel_id=1, source_target_pairs={{16,0},{32,16},{48,32},{64,48},{80,64},{96,80},{112,96},{128,112},... | collective-permute-start | bytes 98312 | tf_op jit(solution)/shard_map/ppermute | solution.py:36
  130.5 9.5 %collective-permute-start.29 = (f32[2,64,2,32]{1,3,2,0:T(8,128)S(1)}, f32[2,64,2,32]{1,3,2,0:T(8,128)S(1)}, u32[]{:S(2)}, u32[]{:S(2)}) collective-permute-start(f32[2,64,2,32]{1,3,2,0:T(8,128)S(1)} %collective-permute-done.28), channel_id=1, source_target_pairs={{0,16},{16,32},{32,48},{48,64},{64,80},{80,96},{96,112},{112,128},... | collective-permute-start | bytes 98312 | tf_op jit(solution)/shard_map/ppermute | solution.py:36
  138.0 9.5 %collective-permute-start.26 = (f32[2,64,2,32]{1,3,2,0:T(8,128)S(1)}, f32[2,64,2,32]{1,3,2,0:T(8,128)S(1)}, u32[]{:S(2)}, u32[]{:S(2)}) collective-permute-start(f32[2,64,2,32]{1,3,2,0:T(8,128)S(1)} %collective-permute-done.25), channel_id=1, source_target_pairs={{16,0},{32,16},{48,32},{64,48},{80,64},{96,80},{112,96},{128,112},... | collective-permute-start | bytes 98312 | tf_op jit(solution)/shard_map/ppermute | solution.py:36
  147.5 8.9 %collective-permute-start.33 = (f32[2,64,8,32]{1,3,2,0:T(8,128)S(1)}, f32[2,64,8,32]{1,3,2,0:T(8,128)S(1)}, u32[]{:S(2)}, u32[]{:S(2)}) collective-permute-start(f32[2,64,8,32]{1,3,2,0:T(8,128)S(1)} %maximum_select_fusion.3), channel_id=1, source_target_pairs={{0,1},{1,2},{2,3},{3,4},{4,5},{5,6},{6,7},{7,8},{8,9},{9,10},{10,1... | collective-permute-start | bytes 393224 | tf_op jit(solution)/shard_map/ppermute | solution.py:36
  149.5 8.9 %collective-permute-start.30 = (f32[2,64,8,32]{1,3,2,0:T(8,128)S(1)}, f32[2,64,8,32]{1,3,2,0:T(8,128)S(1)}, u32[]{:S(2)}, u32[]{:S(2)}) collective-permute-start(f32[2,64,8,32]{1,3,2,0:T(8,128)S(1)} %maximum_select_fusion.3), channel_id=1, source_target_pairs={{1,0},{2,1},{3,2},{4,3},{5,4},{6,5},{7,6},{8,7},{9,8},{10,9},{11,1... | collective-permute-start | bytes 393224 | tf_op jit(solution)/shard_map/ppermute | solution.py:36
  156.4 9.0 %collective-permute-start.34 = (f32[2,64,8,32]{1,3,2,0:T(8,128)S(1)}, f32[2,64,8,32]{1,3,2,0:T(8,128)}, u32[]{:S(2)}, u32[]{:S(2)}) collective-permute-start(f32[2,64,8,32]{1,3,2,0:T(8,128)S(1)} %collective-permute-done.33), channel_id=1, source_target_pairs={{0,1},{1,2},{2,3},{3,4},{4,5},{5,6},{6,7},{7,8},{8,9},{9,10},{10,1... | collective-permute-start | bytes 393224 | tf_op jit(solution)/shard_map/ppermute | solution.py:36
  158.4 9.0 %collective-permute-start.31 = (f32[2,64,8,32]{1,3,2,0:T(8,128)S(1)}, f32[2,64,8,32]{1,3,2,0:T(8,128)}, u32[]{:S(2)}, u32[]{:S(2)}) collective-permute-start(f32[2,64,8,32]{1,3,2,0:T(8,128)S(1)} %collective-permute-done.30), channel_id=1, source_target_pairs={{1,0},{2,1},{3,2},{4,3},{5,4},{6,5},{7,6},{8,7},{9,8},{10,9},{11,1... | collective-permute-start | bytes 393224 | tf_op jit(solution)/shard_map/ppermute | solution.py:36
  165.4 9.2 %collective-permute-start.35 = (f32[2,64,8,32]{1,3,2,0:T(8,128)}, f32[2,64,8,32]{1,3,2,0:T(8,128)}, u32[]{:S(2)}, u32[]{:S(2)}) collective-permute-start(f32[2,64,8,32]{1,3,2,0:T(8,128)} %collective-permute-done.34), channel_id=1, source_target_pairs={{0,1},{1,2},{2,3},{3,4},{4,5},{5,6},{6,7},{7,8},{8,9},{9,10},{10,1... | collective-permute-start | bytes 393224 | tf_op jit(solution)/shard_map/ppermute | solution.py:36
  167.4 9.0 %collective-permute-start.32 = (f32[2,64,8,32]{1,3,2,0:T(8,128)}, f32[2,64,8,32]{1,3,2,0:T(8,128)}, u32[]{:S(2)}, u32[]{:S(2)}) collective-permute-start(f32[2,64,8,32]{1,3,2,0:T(8,128)} %collective-permute-done.31), channel_id=1, source_target_pairs={{1,0},{2,1},{3,2},{4,3},{5,4},{6,5},{7,6},{8,7},{9,8},{10,9},{11,1... | collective-permute-start | bytes 393224 | tf_op jit(solution)/shard_map/ppermute | solution.py:36
  181.6 5.9 %collective-permute-start.37 = (f32[64,1,64]{0,2,1:T(8,128)S(1)}, f32[64,1,64]{0,2,1:T(8,128)S(1)}, u32[]{:S(2)}, u32[]{:S(2)}) collective-permute-start(f32[64,1,64]{0,2,1:T(8,128)S(1)} %get-tuple-element.58), channel_id=1, source_target_pairs={{0,16},{16,32},{32,48},{48,64},{64,80},{80,96},{96,112},{112,128},... | collective-permute-start | bytes 49160 | tf_op jit(solution)/shard_map/ppermute | solution.py:24
  183.5 9.1 %collective-permute-start.36 = (f32[64,1,64]{0,2,1:T(8,128)S(1)}, f32[64,1,64]{0,2,1:T(8,128)S(1)}, u32[]{:S(2)}, u32[]{:S(2)}) collective-permute-start(f32[64,1,64]{0,2,1:T(8,128)S(1)} %get-tuple-element.59), channel_id=1, source_target_pairs={{16,0},{32,16},{48,32},{64,48},{80,64},{96,80},{112,96},{128,112},... | collective-permute-start | bytes 49160 | tf_op jit(solution)/shard_map/ppermute | solution.py:26
  192.7 5.8 %collective-permute-start.38 = (f32[64,6,1]{0,2,1:T(1,128)S(1)}, f32[64,6,1]{0,2,1:T(1,128)S(1)}, u32[]{:S(2)}, u32[]{:S(2)}) collective-permute-start(f32[64,6,1]{0,2,1:T(1,128)S(1)} %get-tuple-element.48), channel_id=1, source_target_pairs={{1,0},{2,1},{3,2},{4,3},{5,4},{6,5},{7,6},{8,7},{9,8},{10,9},{11,1... | collective-permute-start | bytes 4616 | tf_op jit(solution)/shard_map/ppermute | solution.py:26
  196.6 6.1 %collective-permute-start.39 = (f32[64,6,1]{0,2,1:T(1,128)S(1)}, f32[64,6,1]{0,2,1:T(1,128)S(1)}, u32[]{:S(2)}, u32[]{:S(2)}) collective-permute-start(f32[64,6,1]{0,2,1:T(1,128)S(1)} %get-tuple-element.49), channel_id=1, source_target_pairs={{0,1},{1,2},{2,3},{3,4},{4,5},{5,6},{6,7},{7,8},{8,9},{9,10},{10,1... | collective-permute-start | bytes 4616 | tf_op jit(solution)/shard_map/ppermute | solution.py:24
  202.8 5.9 %collective-permute-start.41 = (f32[64,1,64]{0,2,1:T(8,128)S(1)}, f32[64,1,64]{0,2,1:T(8,128)S(1)}, u32[]{:S(2)}, u32[]{:S(2)}) collective-permute-start(f32[64,1,64]{0,2,1:T(8,128)S(1)} %get-tuple-element.56), channel_id=1, source_target_pairs={{0,16},{16,32},{32,48},{48,64},{64,80},{80,96},{96,112},{112,128},... | collective-permute-start | bytes 49160 | tf_op jit(solution)/shard_map/ppermute | solution.py:24
  204.8 9.1 %collective-permute-start.40 = (f32[64,1,64]{0,2,1:T(8,128)S(1)}, f32[64,1,64]{0,2,1:T(8,128)S(1)}, u32[]{:S(2)}, u32[]{:S(2)}) collective-permute-start(f32[64,1,64]{0,2,1:T(8,128)S(1)} %get-tuple-element.57), channel_id=1, source_target_pairs={{16,0},{32,16},{48,32},{64,48},{80,64},{96,80},{112,96},{128,112},... | collective-permute-start | bytes 49160 | tf_op jit(solution)/shard_map/ppermute | solution.py:26
  213.9 4.3 %collective-permute-start.42 = (f32[64,6,1]{0,2,1:T(1,128)S(1)}, f32[64,6,1]{0,2,1:T(1,128)S(1)}, u32[]{:S(2)}, u32[]{:S(2)}) collective-permute-start(f32[64,6,1]{0,2,1:T(1,128)S(1)} %get-tuple-element.46), channel_id=1, source_target_pairs={{1,0},{2,1},{3,2},{4,3},{5,4},{6,5},{7,6},{8,7},{9,8},{10,9},{11,1... | collective-permute-start | bytes 4616 | tf_op jit(solution)/shard_map/ppermute | solution.py:26
  215.8 6.1 %collective-permute-start.43 = (f32[64,6,1]{0,2,1:T(1,128)S(1)}, f32[64,6,1]{0,2,1:T(1,128)S(1)}, u32[]{:S(2)}, u32[]{:S(2)}) collective-permute-start(f32[64,6,1]{0,2,1:T(1,128)S(1)} %get-tuple-element.47), channel_id=1, source_target_pairs={{0,1},{1,2},{2,3},{3,4},{4,5},{5,6},{6,7},{7,8},{8,9},{9,10},{10,1... | collective-permute-start | bytes 4616 | tf_op jit(solution)/shard_map/ppermute | solution.py:24
  222.5 6.2 %collective-permute-start.45 = (f32[64,1,128]{0,2,1:T(8,128)S(1)}, f32[64,1,128]{0,2,1:T(8,128)S(1)}, u32[]{:S(2)}, u32[]{:S(2)}) collective-permute-start(f32[64,1,128]{0,2,1:T(8,128)S(1)} %get-tuple-element.38), channel_id=1, source_target_pairs={{0,16},{16,32},{32,48},{48,64},{64,80},{80,96},{96,112},{112,128},... | collective-permute-start | bytes 98312 | tf_op jit(solution)/shard_map/ppermute | solution.py:24
  224.4 9.5 %collective-permute-start.44 = (f32[64,1,128]{0,2,1:T(8,128)S(1)}, f32[64,1,128]{0,2,1:T(8,128)S(1)}, u32[]{:S(2)}, u32[]{:S(2)}) collective-permute-start(f32[64,1,128]{0,2,1:T(8,128)S(1)} %get-tuple-element.39), channel_id=1, source_target_pairs={{16,0},{32,16},{48,32},{64,48},{80,64},{96,80},{112,96},{128,112},... | collective-permute-start | bytes 98312 | tf_op jit(solution)/shard_map/ppermute | solution.py:26
  233.9 4.3 %collective-permute-start.46 = (f32[64,10,1]{0,2,1:T(1,128)S(1)}, f32[64,10,1]{0,2,1:T(1,128)S(1)}, u32[]{:S(2)}, u32[]{:S(2)}) collective-permute-start(f32[64,10,1]{0,2,1:T(1,128)S(1)} %get-tuple-element.26), channel_id=1, source_target_pairs={{1,0},{2,1},{3,2},{4,3},{5,4},{6,5},{7,6},{8,7},{9,8},{10,9},{11,1... | collective-permute-start | bytes 7688 | tf_op jit(solution)/shard_map/ppermute | solution.py:26
  235.9 6.1 %collective-permute-start.47 = (f32[64,10,1]{0,2,1:T(1,128)S(1)}, f32[64,10,1]{0,2,1:T(1,128)S(1)}, u32[]{:S(2)}, u32[]{:S(2)}) collective-permute-start(f32[64,10,1]{0,2,1:T(1,128)S(1)} %get-tuple-element.27), channel_id=1, source_target_pairs={{0,1},{1,2},{2,3},{3,4},{4,5},{5,6},{6,7},{7,8},{8,9},{9,10},{10,1... | collective-permute-start | bytes 7688 | tf_op jit(solution)/shard_map/ppermute | solution.py:24
  242.5 6.2 %collective-permute-start.49 = (f32[64,1,128]{0,2,1:T(8,128)S(1)}, f32[64,1,128]{0,2,1:T(8,128)S(1)}, u32[]{:S(2)}, u32[]{:S(2)}) collective-permute-start(f32[64,1,128]{0,2,1:T(8,128)S(1)} %get-tuple-element.36), channel_id=1, source_target_pairs={{0,16},{16,32},{32,48},{48,64},{64,80},{80,96},{96,112},{112,128},... | collective-permute-start | bytes 98312 | tf_op jit(solution)/shard_map/ppermute | solution.py:24
  244.4 9.5 %collective-permute-start.48 = (f32[64,1,128]{0,2,1:T(8,128)S(1)}, f32[64,1,128]{0,2,1:T(8,128)S(1)}, u32[]{:S(2)}, u32[]{:S(2)}) collective-permute-start(f32[64,1,128]{0,2,1:T(8,128)S(1)} %get-tuple-element.37), channel_id=1, source_target_pairs={{16,0},{32,16},{48,32},{64,48},{80,64},{96,80},{112,96},{128,112},... | collective-permute-start | bytes 98312 | tf_op jit(solution)/shard_map/ppermute | solution.py:26
  253.9 4.3 %collective-permute-start.50 = (f32[64,10,1]{0,2,1:T(1,128)S(1)}, f32[64,10,1]{0,2,1:T(1,128)S(1)}, u32[]{:S(2)}, u32[]{:S(2)}) collective-permute-start(f32[64,10,1]{0,2,1:T(1,128)S(1)} %get-tuple-element.24), channel_id=1, source_target_pairs={{1,0},{2,1},{3,2},{4,3},{5,4},{6,5},{7,6},{8,7},{9,8},{10,9},{11,1... | collective-permute-start | bytes 7688 | tf_op jit(solution)/shard_map/ppermute | solution.py:26
  255.8 6.1 %collective-permute-start.51 = (f32[64,10,1]{0,2,1:T(1,128)S(1)}, f32[64,10,1]{0,2,1:T(1,128)S(1)}, u32[]{:S(2)}, u32[]{:S(2)}) collective-permute-start(f32[64,10,1]{0,2,1:T(1,128)S(1)} %get-tuple-element.25), channel_id=1, source_target_pairs={{0,1},{1,2},{2,3},{3,4},{4,5},{5,6},{6,7},{7,8},{8,9},{9,10},{10,1... | collective-permute-start | bytes 7688 | tf_op jit(solution)/shard_map/ppermute | solution.py:24
  262.5 6.2 %collective-permute-start.53 = (f32[64,1,128]{0,2,1:T(8,128)S(1)}, f32[64,1,128]{0,2,1:T(8,128)S(1)}, u32[]{:S(2)}, u32[]{:S(2)}) collective-permute-start(f32[64,1,128]{0,2,1:T(8,128)S(1)} %get-tuple-element.34), channel_id=1, source_target_pairs={{0,16},{16,32},{32,48},{48,64},{64,80},{80,96},{96,112},{112,128},... | collective-permute-start | bytes 98312 | tf_op jit(solution)/shard_map/ppermute | solution.py:24
  264.4 9.5 %collective-permute-start.52 = (f32[64,1,128]{0,2,1:T(8,128)S(1)}, f32[64,1,128]{0,2,1:T(8,128)S(1)}, u32[]{:S(2)}, u32[]{:S(2)}) collective-permute-start(f32[64,1,128]{0,2,1:T(8,128)S(1)} %get-tuple-element.35), channel_id=1, source_target_pairs={{16,0},{32,16},{48,32},{64,48},{80,64},{96,80},{112,96},{128,112},... | collective-permute-start | bytes 98312 | tf_op jit(solution)/shard_map/ppermute | solution.py:26
  273.9 5.2 %collective-permute-start.54 = (f32[64,10,1]{0,2,1:T(1,128)S(1)}, f32[64,10,1]{0,2,1:T(1,128)S(1)}, u32[]{:S(2)}, u32[]{:S(2)}) collective-permute-start(f32[64,10,1]{0,2,1:T(1,128)S(1)} %get-tuple-element.22), channel_id=1, source_target_pairs={{1,0},{2,1},{3,2},{4,3},{5,4},{6,5},{7,6},{8,7},{9,8},{10,9},{11,1... | collective-permute-start | bytes 7688 | tf_op jit(solution)/shard_map/ppermute | solution.py:26
  275.8 6.1 %collective-permute-start.55 = (f32[64,10,1]{0,2,1:T(1,128)S(1)}, f32[64,10,1]{0,2,1:T(1,128)S(1)}, u32[]{:S(2)}, u32[]{:S(2)}) collective-permute-start(f32[64,10,1]{0,2,1:T(1,128)S(1)} %get-tuple-element.23), channel_id=1, source_target_pairs={{0,1},{1,2},{2,3},{3,4},{4,5},{5,6},{6,7},{7,8},{8,9},{9,10},{10,1... | collective-permute-start | bytes 7688 | tf_op jit(solution)/shard_map/ppermute | solution.py:24
where the time goes:
time: 285 us; the launch traced here: 283 us
  starting transfers between devices  162 us (57%)
  waiting for transfers between devices  107 us (38%)
  other arithmetic  9.81 us (3%)
    ppermute x22, starting transfers between devices, extended_2(): lax.ppermute(head, axis, [((i + 1) % count, i) for i in range(ends)])  60.4 us
    ppermute x22, starting transfers between devices, extended_2(): lax.ppermute(tail, axis, [(i, (i + 1) % count) for i in range(ends)])  59.3 us
    ppermute x22, waiting for transfers between devices, extended_2(): lax.ppermute(head, axis, [((i + 1) % count, i) for i in range(ends)])  53.7 us
    ppermute x12, starting transfers between devices, passed_along(): return lax.ppermute(block, axis, route)  42.7 us
    ppermute x22, waiting for transfers between devices, extended_2(): lax.ppermute(tail, axis, [(i, (i + 1) % count) for i in range(ends)])  36.7 us
    ppermute x12, waiting for transfers between devices, passed_along(): return lax.ppermute(block, axis, route)  16.3 us
  transfers between devices with their start and end apart: 56, of which 30 were waited for; matrix products, arithmetic and copies ran while one was open for 1% of the time, Pallas kernels for 0%

commit v1 on v0

v1 whole, which is shorter than its diff:
```python
import functools

import jax
import jax.numpy as jnp
from jax import lax
from jax.experimental import pallas as pl
from jax.experimental.pallas import tpu as pltpu
from jax.sharding import PartitionSpec as P


MESH = pl.DeviceIdType.MESH
UPPER = 2.0


def chebyshev_numbers(low):
    mid = (UPPER + low) / 2.0
    half = (UPPER - low) / 2.0
    return mid, half, mid / half


MID, HALF, RATIO = chebyshev_numbers(0.3)
P_ONE = 1.0 / RATIO
P_TWO = 1.0 / (2.0 * RATIO - P_ONE)
BETA = 2.0 * P_TWO / HALF
ALPHA = 1.0 + P_TWO * P_ONE + BETA * (MID - 1.0)
MID2, HALF2, RATIO2 = chebyshev_numbers(0.05)
COARSE = 6

FINE = (8, 80)
POST = (12, 72)
ONE = (12, 40)
OWN = (16, 64)
OWN1 = (16, 32)
TWO = (8, 48)


def kernel(
    f_in, h_in, sol_out, res_out,
    S, G, DD, D, FP, V, DL, PE,
    G1, D1, DD1, OP, V1, DL1, CE,
    WG, WA, WB, WR, WV, QG, QD, AG, AD,
    TS, RS,
    s_fine, r_fine, s_one, r_one, s_op, r_op, s_q, r_q, s_a, r_a,
):
    gx, gy = lax.axis_index("gx"), lax.axis_index("gy")
    nx, ny = lax.axis_size("gx"), lax.axis_size("gy")
    group, pos = gx // 4, lax.rem(gx, 4)

    lane = lax.broadcasted_iota(jnp.int32, (8, 128), 1)
    level = lax.rem(lane, 64)

    def like(mask, value):
        return jnp.broadcast_to(mask[0:1], value.shape)

    def first(value, a, b):
        return jnp.where(like(lane < 64, value), a, b)

    def swap(value):
        return pltpu.roll(value, 64, 1)

    def vertical(c):
        below = jnp.where(like(level > 0, c), pltpu.roll(c, 1, 1), 0.0)
        above = jnp.where(like(level < 63, c), pltpu.roll(c, 127, 1), 0.0)
        return below + above

    def rows(ref, i, span, shift=0):
        return ref[i, pl.ds(span[0] + shift, span[1]), :]

    def beside(ref, i, span, c):
        mixed = first(c, rows(ref, i, span, 1), rows(ref, i, span, -1))
        return rows(ref, i - 1, span) + rows(ref, i + 1, span) + swap(c + mixed)

    def coupled(ref, i, span, c, weight):
        flat = beside(ref, i, span, c)
        if weight != 1.0:
            flat = weight * flat
        return 2.0 * vertical(c) + flat

    def put(ref, i, span, value):
        ref[i, pl.ds(span[0], span[1]), :] = value

    def loop(lo, hi, body, unroll=2):
        def step(i, carry):
            body(i)
            return carry

        lax.fori_loop(lo, hi, step, 0, unroll=unroll)

    def at(dx, dy):
        return (lax.rem(gx + dx + nx, nx), lax.rem(gy + dy + ny, ny))

    mates = [4 * group + lax.rem(pos + k, 4) for k in range(4)]
    edges = [lax.rem(4 * group + nx - 1, nx), lax.rem(4 * group + 4, nx)]
    ys = [gy, lax.rem(gy + 1, ny), lax.rem(gy + ny - 1, ny)]

    barrier = pltpu.get_barrier_semaphore()

    def greet(x, y):
        pl.semaphore_signal(barrier, inc=1, device_id=(x, y), device_id_type=MESH)

    for k in range(4):
        for dy in range(3):
            if (k, dy) != (0, 0):
                greet(mates[k], ys[dy])

    @pl.when(pos == 0)
    def _():
        for k in range(4):
            for dy in range(3):
                greet(lax.rem(4 * group + nx - 4 + k, nx), ys[dy])

    @pl.when(pos == 3)
    def _():
        for k in range(4):
            for dy in range(3):
                greet(lax.rem(4 * group + 4 + k, nx), ys[dy])

    def copy(src, dst, send, recv, x, y):
        return pltpu.make_async_remote_copy(
            src_ref=src, dst_ref=dst, send_sem=send, recv_sem=recv,
            device_id=(x, y), device_id_type=MESH,
        )

    def halo_copies(ref, field, width, planes, interior):
        lo, hi = 4, 4 + planes
        xs = {1: (hi - width, lo - width), -1: (lo, hi), 0: (lo, lo)}
        top = 16 + interior
        yr = {1: (top - 8, 8), -1: (16, top), 0: (16, 16)}
        out = []
        for n, (dx, dy) in enumerate(
            [(0, 1), (0, -1), (1, 0), (-1, 0), (1, 1), (1, -1), (-1, 1), (-1, -1)]
        ):
            wide = width if dx else planes
            tall = 8 if dy else interior
            x, y = at(dx, dy)
            out.append(
                copy(
                    ref.at[pl.ds(xs[dx][0], wide), pl.ds(yr[dy][0], tall)],
                    ref.at[pl.ds(xs[dx][1], wide), pl.ds(yr[dy][1], tall)],
                    s_fine.at[field, n], r_fine.at[field, n], x, y,
                )
            )
        return out

    halo_g = halo_copies(G, 0, 3, 8, 64)
    halo_d = halo_copies(D, 1, 4, 8, 64)
    halo_g1 = halo_copies(G1, 2, 3, 4, 32)

    spans = [((16, 32), (16, 32)), ((40, 8), (8, 8)), ((16, 8), (48, 8))]

    def block_copies(q, a, field):
        out = []
        for k in range(4):
            for dy in range(3):
                if (k, dy) != (0, 0):
                    src, dst = spans[dy]
                    out.append(
                        copy(
                            q.at[0, pl.ds(*src)], q.at[k, pl.ds(*dst)],
                            s_q.at[field, k, dy], r_q.at[field, k, dy], mates[k], ys[dy],
                        )
                    )
        far = []
        for e in range(2):
            for dy in range(3):
                src, dst = spans[dy]
                far.append(
                    copy(
                        q.at[0, pl.ds(*src)], a.at[pos, pl.ds(*dst)],
                        s_a.at[field, e, dy], r_a.at[field, pos, dy], edges[e], ys[dy],
                    )
                )
        return out, far

    def far_arrivals(q, a, field):
        return [
            copy(
                q.at[0, pl.ds(*spans[dy][0])], a.at[s, pl.ds(*spans[dy][1])],
                s_a.at[field, 0, dy], r_a.at[field, s, dy], edges[0], ys[dy],
            )
            for s in range(4)
            for dy in range(3)
        ]

    q_g, a_g = block_copies(QG, AG, 0)
    q_d, a_d = block_copies(QD, AD, 1)

    def turned(ref, k):
        both = jnp.concatenate(
            [ref[pl.ds(2 * k, 64, stride=8), :], ref[pl.ds(2 * k + 1, 64, stride=8), :]], axis=0
        )
        TS[k] = both.T
        even = TS[k, pl.ds(0, 64, stride=2), :]
        odd = TS[k, pl.ds(1, 64, stride=2), :]
        return first(even, even, swap(odd)), first(even, swap(even), odd)

    def packed(value, k, count):
        dup = (value + swap(value)) * 0.25
        RS[k, pl.ds(0, count), :] = dup
        even = RS[k, pl.ds(0, count // 2, stride=2), :]
        odd = RS[k, pl.ds(1, count // 2, stride=2), :]
        return first(even, even, odd)

    coarse = []
    for k in range(4):
        s_a_, s_b_ = turned(h_in, k)
        put(DD, 4 + 2 * k, OWN, 8.0 + s_a_)
        put(DD, 5 + 2 * k, OWN, 8.0 + s_b_)
        put(G, 4 + 2 * k, OWN, 1.0 / (8.0 + s_a_))
        put(G, 5 + 2 * k, OWN, 1.0 / (8.0 + s_b_))
        s_one_ = packed(s_a_ + s_b_, k, 64)
        DD1[k] = 5.0 + s_one_
        put(G1, 4 + k, OWN1, 1.0 / (5.0 + s_one_))
        coarse.append(s_one_)
    two = []
    for k in range(2):
        both = coarse[2 * k] + coarse[2 * k + 1]
        two.append(1.0 / (4.25 + (both + swap(both)) * 0.25))
    put(QG, 0, OWN1, first(two[0], two[0], two[1]))

    pl.semaphore_wait(barrier, 17)
    for c in halo_g:
        c.start()

    for k in range(4):
        f_a, f_b = turned(f_in, k)
        put(D, 4 + 2 * k, OWN, rows(G, 4 + 2 * k, OWN) * f_a * (1.0 / MID))
        put(D, 5 + 2 * k, OWN, rows(G, 5 + 2 * k, OWN) * f_b * (1.0 / MID))
    for c in halo_d:
        c.start()
    for c in halo_g1:
        c.start()
    for c in q_g + a_g:
        c.start()

    def clear(ref, planes, span):
        zero = jnp.zeros((span[1], 128), jnp.float32)
        for i in planes:
            put(ref, i, span, zero)

    def inverse(i, span):
        g = rows(G, i, span)
        put(DD, i, span, jnp.where(g > 0.0, 1.0 / jnp.where(g > 0.0, g, 1.0), 0.0))

    def fine_pre(i):
        c = rows(D, i, FINE)
        n = rows(G, i, FINE) * coupled(D, i, FINE, c, 1.0)
        put(FP, i, FINE, ALPHA * c + BETA * n)

    def fine_rest(i):
        c = rows(FP, i, FINE)
        return rows(DD, i, FINE) * (MID * rows(D, i, FINE) - c) + coupled(FP, i, FINE, c, 1.0)

    def target_one(k):
        i = 2 * k - 4
        total = fine_rest(i) + fine_rest(i + 1)
        put(D1, k, ONE, rows(G1, k, ONE) * packed(total, lax.rem(k, 4), 80) * (1.0 / MID))

    for h in (halo_g, halo_d, halo_g1):
        for c in h[:2]:
            c.wait_recv()

    @pl.when(gy == 0)
    def _():
        clear(G, range(4, 12), (8, 8))
        clear(D, range(4, 12), (8, 8))
        clear(G1, range(4, 8), (8, 8))

    @pl.when(gy == ny - 1)
    def _():
        clear(G, range(4, 12), (80, 8))
        clear(D, range(4, 12), (80, 8))
        clear(G1, range(4, 8), (48, 8))

    def inverse_y(i):
        inverse(i, (8, 8))
        inverse(i, (80, 8))

    loop(4, 12, inverse_y)
    loop(5, 11, fine_pre)
    loop(5, 7, target_one, 2)
    ready = []
    for n, (dx, to) in enumerate([(1, 1), (-1, 9)]):
        x, y = at(dx, 0)
        ready.append(
            copy(
                D1.at[pl.ds(5, 2), pl.ds(8, 48)], D1.at[pl.ds(to, 2), pl.ds(8, 48)],
                s_one.at[n], r_one.at[n], x, y,
            )
        )
    for c in ready:
        c.start()

    for h in (halo_g, halo_d, halo_g1):
        for c in h[2:]:
            c.wait_recv()

    @pl.when(gy == 0)
    def _():
        for planes in (range(0, 4), range(12, 16)):
            clear(G, planes, (8, 8))
            clear(D, planes, (8, 8))
        clear(G1, list(range(0, 4)) + list(range(8, 12)), (8, 8))

    @pl.when(gy == ny - 1)
    def _():
        for planes in (range(0, 4), range(12, 16)):
            clear(G, planes, (80, 8))
            clear(D, planes, (80, 8))
        clear(G1, list(range(0, 4)) + list(range(8, 12)), (48, 8))

    @pl.when(gx == 0)
    def _():
        clear(G, range(0, 4), FINE)
        clear(D, range(0, 4), FINE)
        clear(G1, range(0, 4), TWO)

    @pl.when(gx == nx - 1)
    def _():
        clear(G, range(12, 16), FINE)
        clear(D, range(12, 16), FINE)
        clear(G1, range(8, 12), TWO)

    for i in (2, 3, 12, 13):
        inverse(i, FINE)
    loop(1, 5, fine_pre)
    loop(11, 15, fine_pre)
    loop(3, 5, target_one, 2)
    loop(7, 9, target_one, 2)

    for c in ready:
        c.wait_recv()

    @pl.when(gx == 0)
    def _():
        clear(D1, range(0, 3), TWO)

    @pl.when(gx == nx - 1)
    def _():
        clear(D1, range(9, 12), TWO)

    def one_pre(i):
        c = rows(D1, i, ONE)
        n = rows(G1, i, ONE) * coupled(D1, i, ONE, c, 0.25)
        put(OP, i, ONE, ALPHA * c + BETA * n)

    def one_rest(k):
        i = 4 + k
        c = rows(OP, i, OWN1)
        return DD1[k] * (MID * rows(D1, i, OWN1) - c) + coupled(OP, i, OWN1, c, 0.25)

    loop(3, 9, one_pre)
    both = [one_rest(0) + one_rest(1), one_rest(2) + one_rest(3)]
    both = [(b + swap(b)) * (0.25 / MID2) for b in both]
    put(QD, 0, OWN1, rows(QG, 0, OWN1) * first(both[0], both[0], both[1]))
    for c in q_d + a_d:
        c.start()
    moved = []
    for n, (dx, frm, to) in enumerate([(1, 4, 0), (-1, 6, 10)]):
        x, y = at(dx, 0)
        moved.append(
            copy(
                OP.at[pl.ds(frm, 2), pl.ds(8, 48)], OP.at[pl.ds(to, 2), pl.ds(8, 48)],
                s_op.at[n], r_op.at[n], x, y,
            )
        )
    for c in moved:
        c.start()
    one_pre(2)
    one_pre(9)

    for c in halo_g + halo_d + halo_g1 + q_g + a_g + ready:
        c.wait_send()
    for c in q_g:
        c.wait_recv()

    @pl.when((pos == 0) | (pos == 3))
    def _():
        for c in far_arrivals(QG, AG, 0):
            c.wait_recv()

    def assemble(q, a, write):
        for s in range(4):
            own = rows(q, lax.rem(pos + 4 - s, 4), TWO)
            far = rows(a, s, TWO)
            write(2 * s, first(own, own, swap(far)))
            write(2 * s + 1, first(own, swap(own), far))

    def write_g(i, value):
        put(WG, i, TWO, value)

    assemble(QG, AG, write_g)
    clear(WA, (0, 9), TWO)
    clear(WB, (0, 9), TWO)

    at_row = lax.broadcasted_iota(jnp.int32, (48, 128), 0)
    cut_low = (lax.rem(gy, 4) == 0).astype(jnp.float32)
    cut_high = (lax.rem(gy, 4) == 3).astype(jnp.float32)
    keep_up = 1.0 - jnp.where(at_row == 8, cut_low, 0.0) - jnp.where(at_row == 40, cut_high, 0.0)
    keep_down = 1.0 - jnp.where(at_row == 7, cut_low, 0.0) - jnp.where(at_row == 39, cut_high, 0.0)
    WR[8, pl.ds(8, 48), :] = keep_up
    WR[9, pl.ds(8, 48), :] = keep_down

    for c in q_d:
        c.wait_recv()

    @pl.when((pos == 0) | (pos == 3))
    def _():
        for c in far_arrivals(QD, AD, 1):
            c.wait_recv()

    def write_d(i, value):
        put(WA, i + 1, TWO, value)
        put(WV, i, TWO, value)
        put(WR, i, TWO, MID2 * value)

    assemble(QD, AD, write_d)

    @pl.when(gy == 0)
    def _():
        clear(WG, range(8), (8, 8))
        clear(WA, range(1, 9), (8, 8))
        clear(WV, range(8), (8, 8))
        clear(WR, range(8), (8, 8))

    @pl.when(gy == ny - 1)
    def _():
        clear(WG, range(8), (48, 8))
        clear(WA, range(1, 9), (48, 8))
        clear(WV, range(8), (48, 8))
        clear(WR, range(8), (48, 8))

    p_last = 1.0 / RATIO2
    for sweep in range(COARSE - 1):
        now, later = (WA, WB) if sweep % 2 == 0 else (WB, WA)
        p_next = 1.0 / (2.0 * RATIO2 - p_last)
        keep, gain = p_next * p_last, 2.0 * p_next / HALF2
        p_last = p_next
        final = sweep == COARSE - 2

        def relax(x, now=now, later=later, keep=keep, gain=gain, final=final):
            c = rows(now, x + 1, TWO)
            flat = rows(now, x, TWO) + rows(now, x + 2, TWO)
            flat = flat + rows(WR, 8, TWO) * rows(now, x + 1, TWO, -1)
            flat = flat + rows(WR, 9, TWO) * rows(now, x + 1, TWO, 1)
            n = rows(WG, x, TWO) * (2.0 * vertical(c) + 0.0625 * flat)
            rest = rows(WR, x, TWO) - c + n
            d = keep * c + gain * rest
            if not final:
                put(WR, x, TWO, rest)
                put(later, x + 1, TWO, d)
            put(WV, x, TWO, rows(WV, x, TWO) + d)

        loop(0, 8, relax)

    for k in range(6):
        x = 2 * pos + k - 2
        outside = (x < 0) | (x > 7)
        c = rows(WV, lax.rem(x + 8, 8), TWO)
        half = jnp.where(outside, 1, 0)
        value = jnp.where(like(lane // 64, c) == half, c, swap(c))
        put(CE, k, TWO, value)

    @pl.when(gx == 0)
    def _():
        clear(CE, (0, 1), TWO)

    @pl.when(gx == nx - 1)
    def _():
        clear(CE, (4, 5), TWO)

    for c in moved:
        c.wait_recv()

    @pl.when(gx == 0)
    def _():
        clear(OP, range(0, 2), TWO)

    @pl.when(gx == nx - 1)
    def _():
        clear(OP, range(10, 12), TWO)

    def one_start(k):
        for i in (2 * k, 2 * k + 1):
            put(V1, i, ONE, rows(OP, i, ONE) + rows(CE, k, ONE))

    def change(v, g, d0, to, span, weight):
        def body(i):
            c = rows(v, i, span)
            n = rows(g, i, span) * coupled(v, i, span, c, weight)
            put(to, i, span, rows(d0, i, span) + (n - c) * (1.0 / MID))

        return body

    def smoothed(v, g, d, i, span, weight):
        c = rows(d, i, span)
        n = rows(g, i, span) * coupled(d, i, span, c, weight)
        return rows(v, i, span) + ALPHA * c + BETA * n

    loop(0, 6, one_start)
    loop(1, 11, change(V1, G1, D1, DL1, ONE, 0.25))

    def one_post(i):
        value = smoothed(V1, G1, DL1, i, ONE, 0.25)
        other = swap(value)
        PE[i - 2, pl.ds(8, 40, stride=2), :] = first(value, value, other)
        PE[i - 2, pl.ds(9, 40, stride=2), :] = first(value, other, value)

    loop(2, 10, one_post)

    def fine_start(k):
        for i in (2 * k, 2 * k + 1):
            put(V, i, POST, rows(FP, i, POST) + rows(PE, k, POST))

    put(V, 1, POST, rows(FP, 1, POST) + rows(PE, 0, POST))
    loop(1, 7, fine_start)
    put(V, 14, POST, rows(FP, 14, POST) + rows(PE, 7, POST))
    loop(2, 14, change(V, G, D, DL, POST, 1.0))

    def fine_post(i):
        put(S, i, POST, smoothed(V, G, DL, i, POST, 1.0))

    loop(3, 13, fine_post)

    def returned(ref, k, a, b):
        TS[k, pl.ds(0, 64, stride=2), :] = first(a, a, swap(b))
        TS[k, pl.ds(1, 64, stride=2), :] = first(a, swap(a), b)
        both = TS[k].T
        ref[pl.ds(2 * k, 64, stride=8), :] = both[:64]
        ref[pl.ds(2 * k + 1, 64, stride=8), :] = both[64:]

    def rest(i):
        c = rows(S, i, OWN)
        return rows(DD, i, OWN) * (MID * rows(D, i, OWN) - c) + coupled(S, i, OWN, c, 1.0)

    for k in range(4):
        returned(sol_out, k, rows(S, 4 + 2 * k, OWN), rows(S, 5 + 2 * k, OWN))
    for k in range(4):
        returned(res_out, k, rest(4 + 2 * k), rest(5 + 2 * k))

    for c in q_d + a_d + moved:
        c.wait_send()


def cycle(forcing, helmholtz):
    shape = forcing.shape
    flat = (shape[0] * shape[1], shape[2])

    def buf(*dims):
        return pltpu.VMEM(dims + (128,), jnp.float32)

    fine, one, two = buf(16, 96), buf(12, 64), buf(8, 64)
    dma = pltpu.SemaphoreType.DMA
    out = jax.ShapeDtypeStruct(flat, jnp.float32)
    vmem = pl.BlockSpec(memory_space=pltpu.VMEM)
    solved, rest = pl.pallas_call(
        kernel,
        out_shape=(out, out),
        in_specs=[vmem, vmem],
        out_specs=(vmem, vmem),
        scratch_shapes=[
            fine, fine, fine, fine, fine, fine, fine, buf(8, 96),
            one, one, buf(4, 32), one, one, one, buf(6, 64),
            two, buf(10, 64), buf(10, 64), buf(10, 64), two, buf(4, 64), buf(4, 64), buf(4, 64), buf(4, 64),
            buf(4, 128), buf(4, 80),
            dma((3, 8)), dma((3, 8)), dma((2,)), dma((2,)), dma((2,)), dma((2,)),
            dma((2, 4, 3)), dma((2, 4, 3)), dma((2, 2, 3)), dma((2, 4, 3)),
        ],
        compiler_params=pltpu.CompilerParams(
            collective_id=0, has_side_effects=True, vmem_limit_bytes=40 * 2**20
        ),
        name="vcycle",
    )(forcing.reshape(flat), helmholtz.reshape(flat))
    return solved.reshape(shape), rest.reshape(shape)


def solution(mesh):
    spec = P(None, "gx", "gy")
    return jax.shard_map(
        cycle, mesh=mesh, in_specs=(spec, spec), out_specs=(spec, spec), check_vma=False
    )
```

time: 285 us -> 45.2 us (0.16)
  the two profiles are of different devices: /device:TPU:230 before, /device:TPU:1 now
where the time goes in v1:
time: 45.2 us; the launch traced here: 45.1 us
  Pallas kernels  41.1 us (91%)
  local copies, waits for them, and re-layouts  3.3 us (7%)
  between operations  0.65 us (1%)
    pallas_call x1, Pallas kernels, cycle(): pl.pallas_call(kernel, out_shape=(out, out), in_specs=[vmem, vmem], out_s...  41.1 us
    unnamed x6, local copies, waits for them, and re-layouts  3.3 us

profile of v1, /device:TPU:1, one launch (start us, length us, event | category | flops | bytes accessed | tf_op | source)
XLA Modules:
  0.0 45.1 jit_solution(3795116411975734384)
XLA Ops:
  0.6 0.0 copy-start
  0.6 0.9 %copy-done = f32[64,8,128]{2,1,0:T(8,128)S(1)} copy-done((f32[64,8,128]{2,1,0:T(8,128)S(1)}, f32[64,8,128]{2,1,0:T(8,128)}, u32[]{:S(2)}) %copy-start) | copy-done | bytes 262168
  1.6 0.0 copy-start.1
  1.6 0.9 %copy-done.1 = f32[64,8,128]{2,1,0:T(8,128)S(1)} copy-done((f32[64,8,128]{2,1,0:T(8,128)S(1)}, f32[64,8,128]{2,1,0:T(8,128)}, u32[]{:S(2)}) %copy-start.1) | copy-done | bytes 262168
  2.5 41.1 %vcycle.1 = (f32[512,128]{1,0:T(8,128)S(1)}, f32[512,128]{1,0:T(8,128)S(1)}) custom-call(f32[512,128]{1,0:T(8,128)S(1)} %bitcast.4, f32[512,128]{1,0:T(8,128)S(1)} %bitcast.5), custom_call_target="tpu_custom_call" | custom-call | tf_op jit(solution)/shard_map/vcycle/pallas_call | solution.py:556
  43.7 0.7 %copy.6 = f32[64,8,128]{2,1,0:T(8,128)} copy(f32[64,8,128]{2,1,0:T(8,128)S(1)} %bitcast.7) | data formatting | bytes 524288
  44.4 0.7 %copy.7 = f32[64,8,128]{2,1,0:T(8,128)} copy(f32[64,8,128]{2,1,0:T(8,128)S(1)} %bitcast.6) | data formatting | bytes 524288
Async XLA Ops:
  0.6 1.0 %copy-start = (f32[64,8,128]{2,1,0:T(8,128)S(1)}, f32[64,8,128]{2,1,0:T(8,128)}, u32[]{:S(2)}) copy-start(f32[64,8,128]{2,1,0:T(8,128)} %param.2) | copy-start | bytes 786436
  1.6 0.9 %copy-start.1 = (f32[64,8,128]{2,1,0:T(8,128)S(1)}, f32[64,8,128]{2,1,0:T(8,128)}, u32[]{:S(2)}) copy-start(f32[64,8,128]{2,1,0:T(8,128)} %param.3) | copy-start | bytes 786436

commit v2 on v1

--- a/solution.py
+++ b/solution.py
@@ -35,11 +35,12 @@
 
 
 def kernel(
-    f_in, h_in, sol_out, res_out,
+    f_hbm, h_hbm, sol_out, res_out,
     S, G, DD, D, FP, V, DL, PE,
     G1, D1, DD1, OP, V1, DL1, CE,
     WG, WA, WB, WR, WV, QG, QD, AG, AD,
     TS, RS,
+    f_in, h_in, s_in,
     s_fine, r_fine, s_one, r_one, s_op, r_op, s_q, r_q, s_a, r_a,
 ):
     gx, gy = lax.axis_index("gx"), lax.axis_index("gy")
@@ -86,34 +87,101 @@
 
         lax.fori_loop(lo, hi, step, 0, unroll=unroll)
 
+    load_h = pltpu.make_async_copy(h_hbm, h_in, s_in.at[0])
+    load_f = pltpu.make_async_copy(f_hbm, f_in, s_in.at[1])
+    load_h.start()
+    load_f.start()
+
+    groups = nx // 4
+    one, none = jnp.int32(1), jnp.int32(0)
+    has_x = {0: None, 1: gx < nx - 1, -1: gx > 0}
+    has_y = {0: None, 1: gy < ny - 1, -1: gy > 0}
+    has_group = {1: group < groups - 1, -1: group > 0}
+
+    def both_of(a, b):
+        if a is None or b is None:
+            return b if a is None else a
+        return a & b
+
+    def when(condition, act):
+        if condition is None:
+            act()
+        else:
+            pl.when(condition)(act)
+
     def at(dx, dy):
         return (lax.rem(gx + dx + nx, nx), lax.rem(gy + dy + ny, ny))
 
     mates = [4 * group + lax.rem(pos + k, 4) for k in range(4)]
     edges = [lax.rem(4 * group + nx - 1, nx), lax.rem(4 * group + 4, nx)]
-    ys = [gy, lax.rem(gy + 1, ny), lax.rem(gy + ny - 1, ny)]
+    sides = (0, 1, -1)
+    ys = [lax.rem(gy + d + ny, ny) for d in sides]
 
     barrier = pltpu.get_barrier_semaphore()
 
     def greet(x, y):
         pl.semaphore_signal(barrier, inc=1, device_id=(x, y), device_id_type=MESH)
 
-    for k in range(4):
-        for dy in range(3):
+    def greet_column(dy):
+        for k in range(4):
             if (k, dy) != (0, 0):
                 greet(mates[k], ys[dy])
 
-    @pl.when(pos == 0)
-    def _():
-        for k in range(4):
-            for dy in range(3):
+        @pl.when((pos == 0) & has_group[-1])
+        def _():
+            for k in range(4):
                 greet(lax.rem(4 * group + nx - 4 + k, nx), ys[dy])
 
-    @pl.when(pos == 3)
-    def _():
-        for k in range(4):
-            for dy in range(3):
+        @pl.when((pos == 3) & has_group[1])
+        def _():
+            for k in range(4):
                 greet(lax.rem(4 * group + 4 + k, nx), ys[dy])
+
+    for dy in range(3):
+        when(has_y[sides[dy]], functools.partial(greet_column, dy))
+
+    columns = one + jnp.where(gy > 0, one, none) + jnp.where(gy < ny - 1, one, none)
+    blocks = 4 + jnp.where(has_group[1], one, none) + jnp.where(has_group[-1], one, none)
+    guests = blocks * columns - 1
+
+    def clear(ref, planes, span):
+        zero = jnp.zeros((span[1], 128), jnp.float32)
+        for i in planes:
+            put(ref, i, span, zero)
+
+    @pl.when(gy == 0)
+    def _():
+        for ref, count in ((G, 16), (D, 16), (G1, 12)):
+            clear(ref, range(count), (8, 8))
+        for ref in (QG, QD):
+            clear(ref, range(4), (8, 8))
+        for ref in (AG, AD):
+            clear(ref, range(4), (8, 8))
+
+    @pl.when(gy == ny - 1)
+    def _():
+        for ref, count, start in ((G, 16, 80), (D, 16, 80), (G1, 12, 48)):
+            clear(ref, range(count), (start, 8))
+        for ref in (QG, QD):
+            clear(ref, range(4), (48, 8))
+        for ref in (AG, AD):
+            clear(ref, range(4), (48, 8))
+
+    @pl.when(gx == 0)
+    def _():
+        clear(G, range(0, 4), FINE)
+        clear(D, range(0, 4), FINE)
+        clear(G1, range(0, 4), TWO)
+        clear(D1, range(0, 3), TWO)
+        clear(OP, range(0, 2), TWO)
+
+    @pl.when(gx == nx - 1)
+    def _():
+        clear(G, range(12, 16), FINE)
+        clear(D, range(12, 16), FINE)
+        clear(G1, range(8, 12), TWO)
+        clear(D1, range(9, 12), TWO)
+        clear(OP, range(10, 12), TWO)
 
     def copy(src, dst, send, recv, x, y):
         return pltpu.make_async_remote_copy(
@@ -133,13 +201,15 @@
             wide = width if dx else planes
             tall = 8 if dy else interior
             x, y = at(dx, dy)
-            out.append(
+            out.append((
+                both_of(has_x[dx], has_y[dy]),
+                both_of(has_x[-dx], has_y[-dy]),
                 copy(
                     ref.at[pl.ds(xs[dx][0], wide), pl.ds(yr[dy][0], tall)],
                     ref.at[pl.ds(xs[dx][1], wide), pl.ds(yr[dy][1], tall)],
                     s_fine.at[field, n], r_fine.at[field, n], x, y,
-                )
-            )
+                ),
+            ))
         return out
 
     halo_g = halo_copies(G, 0, 3, 8, 64)
@@ -154,33 +224,51 @@
             for dy in range(3):
                 if (k, dy) != (0, 0):
                     src, dst = spans[dy]
-                    out.append(
+                    out.append((
+                        has_y[sides[dy]],
+                        has_y[-sides[dy]],
                         copy(
                             q.at[0, pl.ds(*src)], q.at[k, pl.ds(*dst)],
                             s_q.at[field, k, dy], r_q.at[field, k, dy], mates[k], ys[dy],
-                        )
-                    )
+                        ),
+                    ))
         far = []
         for e in range(2):
             for dy in range(3):
                 src, dst = spans[dy]
-                far.append(
+                far.append((
+                    both_of(has_group[(-1, 1)[e]], has_y[sides[dy]]),
+                    None,
                     copy(
                         q.at[0, pl.ds(*src)], a.at[pos, pl.ds(*dst)],
                         s_a.at[field, e, dy], r_a.at[field, pos, dy], edges[e], ys[dy],
-                    )
-                )
+                    ),
+                ))
         return out, far
 
     def far_arrivals(q, a, field):
         return [
-            copy(
+            (None, has_y[-sides[dy]], copy(
                 q.at[0, pl.ds(*spans[dy][0])], a.at[s, pl.ds(*spans[dy][1])],
                 s_a.at[field, 0, dy], r_a.at[field, s, dy], edges[0], ys[dy],
-            )
+            ))
             for s in range(4)
             for dy in range(3)
         ]
+
+    def start(copies):
+        for sends, _, c in copies:
+            when(sends, c.start)
+
+    def wait_send(copies):
+        for sends, _, c in copies:
+            when(sends, c.wait_send)
+
+    def wait_recv(copies):
+        for _, arrives, c in copies:
+            when(arrives, c.wait_recv)
+
+    far_block = ((pos == 0) & has_group[-1]) | ((pos == 3) & has_group[1])
 
     q_g, a_g = block_copies(QG, AG, 0)
     q_d, a_d = block_copies(QD, AD, 1)
@@ -202,6 +290,7 @@
         return first(even, even, odd)
 
     coarse = []
+    load_h.wait()
     for k in range(4):
         s_a_, s_b_ = turned(h_in, k)
         put(DD, 4 + 2 * k, OWN, 8.0 + s_a_)
@@ -218,25 +307,15 @@
         two.append(1.0 / (4.25 + (both + swap(both)) * 0.25))
     put(QG, 0, OWN1, first(two[0], two[0], two[1]))
 
-    pl.semaphore_wait(barrier, 17)
-    for c in halo_g:
-        c.start()
-
+    pl.semaphore_wait(barrier, guests)
+    start(halo_g)
+
+    load_f.wait()
     for k in range(4):
         f_a, f_b = turned(f_in, k)
         put(D, 4 + 2 * k, OWN, rows(G, 4 + 2 * k, OWN) * f_a * (1.0 / MID))
         put(D, 5 + 2 * k, OWN, rows(G, 5 + 2 * k, OWN) * f_b * (1.0 / MID))
-    for c in halo_d:
-        c.start()
-    for c in halo_g1:
-        c.start()
-    for c in q_g + a_g:
-        c.start()
-
-    def clear(ref, planes, span):
-        zero = jnp.zeros((span[1], 128), jnp.float32)
-        for i in planes:
-            put(ref, i, span, zero)
+    start(halo_d + halo_g1 + q_g + a_g)
 
     def inverse(i, span):
         g = rows(G, i, span)
@@ -257,20 +336,7 @@
         put(D1, k, ONE, rows(G1, k, ONE) * packed(total, lax.rem(k, 4), 80) * (1.0 / MID))
 
     for h in (halo_g, halo_d, halo_g1):
-        for c in h[:2]:
-            c.wait_recv()
-
-    @pl.when(gy == 0)
-    def _():
-        clear(G, range(4, 12), (8, 8))
-        clear(D, range(4, 12), (8, 8))
-        clear(G1, range(4, 8), (8, 8))
-
-    @pl.when(gy == ny - 1)
-    def _():
-        clear(G, range(4, 12), (80, 8))
-        clear(D, range(4, 12), (80, 8))
-        clear(G1, range(4, 8), (48, 8))
+        wait_recv(h[:2])
 
     def inverse_y(i):
         inverse(i, (8, 8))
@@ -282,44 +348,18 @@
     ready = []
     for n, (dx, to) in enumerate([(1, 1), (-1, 9)]):
         x, y = at(dx, 0)
-        ready.append(
+        ready.append((
+            has_x[dx],
+            has_x[-dx],
             copy(
                 D1.at[pl.ds(5, 2), pl.ds(8, 48)], D1.at[pl.ds(to, 2), pl.ds(8, 48)],
                 s_one.at[n], r_one.at[n], x, y,
-            )
-        )
-    for c in ready:
-        c.start()
+            ),
+        ))
+    start(ready)
 
     for h in (halo_g, halo_d, halo_g1):
-        for c in h[2:]:
-            c.wait_recv()
-
-    @pl.when(gy == 0)
-    def _():
-        for planes in (range(0, 4), range(12, 16)):
-            clear(G, planes, (8, 8))
-            clear(D, planes, (8, 8))
-        clear(G1, list(range(0, 4)) + list(range(8, 12)), (8, 8))
-
-    @pl.when(gy == ny - 1)
-    def _():
-        for planes in (range(0, 4), range(12, 16)):
-            clear(G, planes, (80, 8))
-            clear(D, planes, (80, 8))
-        clear(G1, list(range(0, 4)) + list(range(8, 12)), (48, 8))
-
-    @pl.when(gx == 0)
-    def _():
-        clear(G, range(0, 4), FINE)
-        clear(D, range(0, 4), FINE)
-        clear(G1, range(0, 4), TWO)
-
-    @pl.when(gx == nx - 1)
-    def _():
-        clear(G, range(12, 16), FINE)
-        clear(D, range(12, 16), FINE)
-        clear(G1, range(8, 12), TWO)
+        wait_recv(h[2:])
 
     for i in (2, 3, 12, 13):
         inverse(i, FINE)
@@ -328,16 +368,7 @@
     loop(3, 5, target_one, 2)
     loop(7, 9, target_one, 2)
 
-    for c in ready:
-        c.wait_recv()
-
-    @pl.when(gx == 0)
-    def _():
-        clear(D1, range(0, 3), TWO)
-
-    @pl.when(gx == nx - 1)
-    def _():
-        clear(D1, range(9, 12), TWO)
+    wait_recv(ready)
 
     def one_pre(i):
         c = rows(D1, i, ONE)
@@ -353,31 +384,28 @@
     both = [one_rest(0) + one_rest(1), one_rest(2) + one_rest(3)]
     both = [(b + swap(b)) * (0.25 / MID2) for b in both]
     put(QD, 0, OWN1, rows(QG, 0, OWN1) * first(both[0], both[0], both[1]))
-    for c in q_d + a_d:
-        c.start()
+    start(q_d + a_d)
     moved = []
     for n, (dx, frm, to) in enumerate([(1, 4, 0), (-1, 6, 10)]):
         x, y = at(dx, 0)
-        moved.append(
+        moved.append((
+            has_x[dx],
+            has_x[-dx],
             copy(
                 OP.at[pl.ds(frm, 2), pl.ds(8, 48)], OP.at[pl.ds(to, 2), pl.ds(8, 48)],
                 s_op.at[n], r_op.at[n], x, y,
-            )
-        )
-    for c in moved:
-        c.start()
+            ),
+        ))
+    start(moved)
     one_pre(2)
     one_pre(9)
 
-    for c in halo_g + halo_d + halo_g1 + q_g + a_g + ready:
-        c.wait_send()
-    for c in q_g:
-        c.wait_recv()
-
-    @pl.when((pos == 0) | (pos == 3))
-    def _():
-        for c in far_arrivals(QG, AG, 0):
-            c.wait_recv()
+    wait_send(halo_g + halo_d + halo_g1 + q_g + a_g + ready)
+    wait_recv(q_g)
+
+    @pl.when(far_block)
+    def _():
+        wait_recv(far_arrivals(QG, AG, 0))
 
     def assemble(q, a, write):
         for s in range(4):
@@ -401,13 +429,11 @@
     WR[8, pl.ds(8, 48), :] = keep_up
     WR[9, pl.ds(8, 48), :] = keep_down
 
-    for c in q_d:
-        c.wait_recv()
-
-    @pl.when((pos == 0) | (pos == 3))
-    def _():
-        for c in far_arrivals(QD, AD, 1):
-            c.wait_recv()
+    wait_recv(q_d)
+
+    @pl.when(far_block)
+    def _():
+        wait_recv(far_arrivals(QD, AD, 1))
 
     def write_d(i, value):
         put(WA, i + 1, TWO, value)
@@ -415,20 +441,6 @@
         put(WR, i, TWO, MID2 * value)
 
     assemble(QD, AD, write_d)
-
-    @pl.when(gy == 0)
-    def _():
-        clear(WG, range(8), (8, 8))
-        clear(WA, range(1, 9), (8, 8))
-        clear(WV, range(8), (8, 8))
-        clear(WR, range(8), (8, 8))
-
-    @pl.when(gy == ny - 1)
-    def _():
-        clear(WG, range(8), (48, 8))
-        clear(WA, range(1, 9), (48, 8))
-        clear(WV, range(8), (48, 8))
-        clear(WR, range(8), (48, 8))
 
     p_last = 1.0 / RATIO2
     for sweep in range(COARSE - 1):
@@ -469,16 +481,7 @@
     def _():
         clear(CE, (4, 5), TWO)
 
-    for c in moved:
-        c.wait_recv()
-
-    @pl.when(gx == 0)
-    def _():
-        clear(OP, range(0, 2), TWO)
-
-    @pl.when(gx == nx - 1)
-    def _():
-        clear(OP, range(10, 12), TWO)
+    wait_recv(moved)
 
     def one_start(k):
         for i in (2 * k, 2 * k + 1):
@@ -538,8 +541,7 @@
     for k in range(4):
         returned(res_out, k, rest(4 + 2 * k), rest(5 + 2 * k))
 
-    for c in q_d + a_d + moved:
-        c.wait_send()
+    wait_send(q_d + a_d + moved)
 
 
 def cycle(forcing, helmholtz):
@@ -556,13 +558,14 @@
     solved, rest = pl.pallas_call(
         kernel,
         out_shape=(out, out),
-        in_specs=[vmem, vmem],
+        in_specs=[pl.BlockSpec(memory_space=pl.ANY)] * 2,
         out_specs=(vmem, vmem),
         scratch_shapes=[
             fine, fine, fine, fine, fine, fine, fine, buf(8, 96),
             one, one, buf(4, 32), one, one, one, buf(6, 64),
             two, buf(10, 64), buf(10, 64), buf(10, 64), two, buf(4, 64), buf(4, 64), buf(4, 64), buf(4, 64),
             buf(4, 128), buf(4, 80),
+            buf(512), buf(512), dma((2,)),
             dma((3, 8)), dma((3, 8)), dma((2,)), dma((2,)), dma((2,)), dma((2,)),
             dma((2, 4, 3)), dma((2, 4, 3)), dma((2, 2, 3)), dma((2, 4, 3)),
         ],

time: 45.2 us -> 37.5 us (0.83)
  the two profiles are of different devices: /device:TPU:1 before, /device:TPU:217 now
where the time goes in v2:
time: 37.5 us; the launch traced here: 37.3 us
  Pallas kernels  33.4 us (89%)
  local copies, waits for them, and re-layouts  3.3 us (9%)
  between operations  0.65 us (2%)
    pallas_call x1, Pallas kernels, cycle(): pl.pallas_call(kernel, out_shape=(out, out), in_specs=[pl.BlockSpec(memor...  33.4 us
    unnamed x6, local copies, waits for them, and re-layouts  3.3 us

profile of v2, /device:TPU:217, one launch (start us, length us, event | category | flops | bytes accessed | tf_op | source)
XLA Modules:
  0.0 37.3 jit_solution(3581273645187754675)
XLA Ops:
  0.6 0.0 copy-start
  0.6 0.9 %copy-done = f32[64,8,128]{2,1,0:T(8,128)S(1)} copy-done((f32[64,8,128]{2,1,0:T(8,128)S(1)}, f32[64,8,128]{2,1,0:T(8,128)}, u32[]{:S(2)}) %copy-start) | copy-done | bytes 262168
  1.6 0.0 copy-start.1
  1.6 0.9 %copy-done.1 = f32[64,8,128]{2,1,0:T(8,128)S(1)} copy-done((f32[64,8,128]{2,1,0:T(8,128)S(1)}, f32[64,8,128]{2,1,0:T(8,128)}, u32[]{:S(2)}) %copy-start.1) | copy-done | bytes 262168
  2.5 33.4 %vcycle.1 = (f32[512,128]{1,0:T(8,128)S(1)}, f32[512,128]{1,0:T(8,128)S(1)}) custom-call(f32[512,128]{1,0:T(8,128)S(1)} %bitcast.4, f32[512,128]{1,0:T(8,128)S(1)} %bitcast.5), custom_call_target="tpu_custom_call" | custom-call | tf_op jit(solution)/shard_map/vcycle/pallas_call | solution.py:558
  35.9 0.7 %copy.6 = f32[64,8,128]{2,1,0:T(8,128)} copy(f32[64,8,128]{2,1,0:T(8,128)S(1)} %bitcast.7) | data formatting | bytes 524288
  36.6 0.7 %copy.7 = f32[64,8,128]{2,1,0:T(8,128)} copy(f32[64,8,128]{2,1,0:T(8,128)S(1)} %bitcast.6) | data formatting | bytes 524288
Async XLA Ops:
  0.6 1.0 %copy-start = (f32[64,8,128]{2,1,0:T(8,128)S(1)}, f32[64,8,128]{2,1,0:T(8,128)}, u32[]{:S(2)}) copy-start(f32[64,8,128]{2,1,0:T(8,128)} %param.2) | copy-start | bytes 786436
  1.6 0.9 %copy-start.1 = (f32[64,8,128]{2,1,0:T(8,128)S(1)}, f32[64,8,128]{2,1,0:T(8,128)}, u32[]{:S(2)}) copy-start(f32[64,8,128]{2,1,0:T(8,128)} %param.3) | copy-start | bytes 786436

commit v3 on v2

--- a/solution.py
+++ b/solution.py
@@ -80,12 +80,12 @@
     def put(ref, i, span, value):
         ref[i, pl.ds(span[0], span[1]), :] = value
 
-    def loop(lo, hi, body, unroll=2):
+    def loop(lo, hi, body, unroll=16):
         def step(i, carry):
             body(i)
             return carry
 
-        lax.fori_loop(lo, hi, step, 0, unroll=unroll)
+        lax.fori_loop(lo, hi, step, 0, unroll=min(unroll, hi - lo))
 
     load_h = pltpu.make_async_copy(h_hbm, h_in, s_in.at[0])
     load_f = pltpu.make_async_copy(f_hbm, f_in, s_in.at[1])
@@ -344,7 +344,7 @@
 
     loop(4, 12, inverse_y)
     loop(5, 11, fine_pre)
-    loop(5, 7, target_one, 2)
+    loop(5, 7, target_one)
     ready = []
     for n, (dx, to) in enumerate([(1, 1), (-1, 9)]):
         x, y = at(dx, 0)
@@ -365,8 +365,8 @@
         inverse(i, FINE)
     loop(1, 5, fine_pre)
     loop(11, 15, fine_pre)
-    loop(3, 5, target_one, 2)
-    loop(7, 9, target_one, 2)
+    loop(3, 5, target_one)
+    loop(7, 9, target_one)
 
     wait_recv(ready)
 
@@ -570,7 +570,7 @@
             dma((2, 4, 3)), dma((2, 4, 3)), dma((2, 2, 3)), dma((2, 4, 3)),
         ],
         compiler_params=pltpu.CompilerParams(
-            collective_id=0, has_side_effects=True, vmem_limit_bytes=40 * 2**20
+            collective_id=0, has_side_effects=True, vmem_limit_bytes=53 * 2**20 + 5 * 2**16
         ),
         name="vcycle",
     )(forcing.reshape(flat), helmholtz.reshape(flat))

time: 37.5 us -> 32.6 us (0.87)
  Pallas kernels: 33.4 us -> 30.5 us
  local copies, waits for them, and re-layouts: 3.3 us -> 1.41 us
    pallas_call x1, Pallas kernels: 33.4 us -> 30.5 us  [cycle(): pl.pallas_call(kernel, out_shape=(out, out), in_specs=[pl.BlockSpec(memor...]
    unnamed x6 -> x2, local copies, waits for them, and re-layouts: 3.3 us -> 1.41 us
where the time goes in v3:
time: 32.6 us; the launch traced here: 32.5 us
  Pallas kernels  30.5 us (94%)
  local copies, waits for them, and re-layouts  1.41 us (4%)
  between operations  0.64 us (2%)
    pallas_call x1, Pallas kernels, cycle(): pl.pallas_call(kernel, out_shape=(out, out), in_specs=[pl.BlockSpec(memor...  30.5 us
    unnamed x2, local copies, waits for them, and re-layouts  1.41 us

profile of v3, /device:TPU:217, one launch (start us, length us, event | category | flops | bytes accessed | tf_op | source)
XLA Modules:
  0.0 32.5 jit_solution(11794149137434101218)
XLA Ops:
  0.6 30.5 %vcycle.1 = (f32[512,128]{1,0:T(8,128)S(1)}, f32[512,128]{1,0:T(8,128)S(1)}) custom-call(f32[512,128]{1,0:T(8,128)} %bitcast.6, f32[512,128]{1,0:T(8,128)} %bitcast.7), custom_call_target="tpu_custom_call" | custom-call | tf_op jit(solution)/shard_map/vcycle/pallas_call | solution.py:558
  31.1 0.7 %copy.6 = f32[64,8,128]{2,1,0:T(8,128)} copy(f32[64,8,128]{2,1,0:T(8,128)S(1)} %bitcast.5) | data formatting | bytes 524288
  31.8 0.7 %copy.7 = f32[64,8,128]{2,1,0:T(8,128)} copy(f32[64,8,128]{2,1,0:T(8,128)S(1)} %bitcast.4) | data formatting | bytes 524288

commit v4 on v3

--- a/solution.py
+++ b/solution.py
@@ -32,6 +32,8 @@
 OWN = (16, 64)
 OWN1 = (16, 32)
 TWO = (8, 48)
+INNER_PRE, INNER, INNER1 = (20, 56), (24, 48), (20, 24)
+ENDS = (((8, 16), (12, 8)), ((72, 16), (44, 8)))
 
 
 def kernel(
@@ -41,7 +43,7 @@
     WG, WA, WB, WR, WV, QG, QD, AG, AD,
     TS, RS,
     f_in, h_in, s_in,
-    s_fine, r_fine, s_one, r_one, s_op, r_op, s_q, r_q, s_a, r_a,
+    s_fine, r_fine, s_x, r_x, s_q, r_q, s_a, r_a,
 ):
     gx, gy = lax.axis_index("gx"), lax.axis_index("gy")
     nx, ny = lax.axis_size("gx"), lax.axis_size("gy")
@@ -67,12 +69,15 @@
     def rows(ref, i, span, shift=0):
         return ref[i, pl.ds(span[0] + shift, span[1]), :]
 
-    def beside(ref, i, span, c):
+    def beside(ref, i, span, c, planes):
         mixed = first(c, rows(ref, i, span, 1), rows(ref, i, span, -1))
-        return rows(ref, i - 1, span) + rows(ref, i + 1, span) + swap(c + mixed)
-
-    def coupled(ref, i, span, c, weight):
-        flat = beside(ref, i, span, c)
+        flat = swap(c + mixed)
+        for step in planes:
+            flat = flat + rows(ref, i + step, span)
+        return flat
+
+    def coupled(ref, i, span, c, weight, planes=(-1, 1)):
+        flat = beside(ref, i, span, c, planes)
         if weight != 1.0:
             flat = weight * flat
         return 2.0 * vertical(c) + flat
@@ -151,8 +156,8 @@
 
     @pl.when(gy == 0)
     def _():
-        for ref, count in ((G, 16), (D, 16), (G1, 12)):
-            clear(ref, range(count), (8, 8))
+        for ref, planes in ((G, range(16)), (D, range(16)), (G1, range(4, 8))):
+            clear(ref, planes, (8, 8))
         for ref in (QG, QD):
             clear(ref, range(4), (8, 8))
         for ref in (AG, AD):
@@ -160,8 +165,8 @@
 
     @pl.when(gy == ny - 1)
     def _():
-        for ref, count, start in ((G, 16, 80), (D, 16, 80), (G1, 12, 48)):
-            clear(ref, range(count), (start, 8))
+        for ref, planes, start in ((G, range(16), 80), (D, range(16), 80), (G1, range(4, 8), 48)):
+            clear(ref, planes, (start, 8))
         for ref in (QG, QD):
             clear(ref, range(4), (48, 8))
         for ref in (AG, AD):
@@ -172,7 +177,8 @@
         clear(G, range(0, 4), FINE)
         clear(D, range(0, 4), FINE)
         clear(G1, range(0, 4), TWO)
-        clear(D1, range(0, 3), TWO)
+        clear(D1, range(0, 4), TWO)
+        clear(FP, range(0, 3), FINE)
         clear(OP, range(0, 2), TWO)
 
     @pl.when(gx == nx - 1)
@@ -180,7 +186,8 @@
         clear(G, range(12, 16), FINE)
         clear(D, range(12, 16), FINE)
         clear(G1, range(8, 12), TWO)
-        clear(D1, range(9, 12), TWO)
+        clear(D1, range(8, 12), TWO)
+        clear(FP, range(13, 16), FINE)
         clear(OP, range(10, 12), TWO)
 
     def copy(src, dst, send, recv, x, y):
@@ -189,14 +196,14 @@
             device_id=(x, y), device_id_type=MESH,
         )
 
-    def halo_copies(ref, field, width, planes, interior):
+    def halo_copies(ref, field, width, planes, interior, count=8):
         lo, hi = 4, 4 + planes
         xs = {1: (hi - width, lo - width), -1: (lo, hi), 0: (lo, lo)}
         top = 16 + interior
         yr = {1: (top - 8, 8), -1: (16, top), 0: (16, 16)}
         out = []
         for n, (dx, dy) in enumerate(
-            [(0, 1), (0, -1), (1, 0), (-1, 0), (1, 1), (1, -1), (-1, 1), (-1, -1)]
+            [(0, 1), (0, -1), (1, 0), (-1, 0), (1, 1), (1, -1), (-1, 1), (-1, -1)][:count]
         ):
             wide = width if dx else planes
             tall = 8 if dy else interior
@@ -212,9 +219,31 @@
             ))
         return out
 
-    halo_g = halo_copies(G, 0, 3, 8, 64)
-    halo_d = halo_copies(D, 1, 4, 8, 64)
-    halo_g1 = halo_copies(G1, 2, 3, 4, 32)
+    halo_g = halo_copies(G, 0, 1, 8, 64)
+    halo_d = halo_copies(D, 1, 2, 8, 64)
+    halo_g1 = halo_copies(G1, 2, 3, 4, 32, 2)
+
+    def plane_copies(ref, field, count, span, right, left):
+        out = []
+        for n, (dx, (frm, to)) in enumerate([(1, right), (-1, left)]):
+            x, y = at(dx, 0)
+            out.append((
+                has_x[dx],
+                has_x[-dx],
+                copy(
+                    ref.at[pl.ds(frm, count), pl.ds(*span)], ref.at[pl.ds(to, count), pl.ds(*span)],
+                    s_x.at[field, n], r_x.at[field, n], x, y,
+                ),
+            ))
+        return out
+
+    near_g1 = plane_copies(G1, 0, 1, TWO, (7, 3), (4, 8))
+    near_d1 = plane_copies(D1, 1, 2, TWO, (6, 2), (4, 8))
+    more_fp = plane_copies(FP, 2, 2, FINE, (9, 1), (5, 13))
+    more_g = plane_copies(G, 3, 1, OWN, (10, 2), (5, 13))
+    more_g1 = plane_copies(G1, 4, 2, TWO, (5, 1), (5, 9))
+    more_d1 = plane_copies(D1, 5, 1, TWO, (5, 1), (6, 10))
+    more_op = plane_copies(OP, 6, 2, TWO, (4, 0), (6, 10))
 
     spans = [((16, 32), (16, 32)), ((40, 8), (8, 8)), ((16, 8), (48, 8))]
 
@@ -307,68 +336,71 @@
         two.append(1.0 / (4.25 + (both + swap(both)) * 0.25))
     put(QG, 0, OWN1, first(two[0], two[0], two[1]))
 
-    pl.semaphore_wait(barrier, guests)
-    start(halo_g)
-
     load_f.wait()
     for k in range(4):
         f_a, f_b = turned(f_in, k)
         put(D, 4 + 2 * k, OWN, rows(G, 4 + 2 * k, OWN) * f_a * (1.0 / MID))
         put(D, 5 + 2 * k, OWN, rows(G, 5 + 2 * k, OWN) * f_b * (1.0 / MID))
-    start(halo_d + halo_g1 + q_g + a_g)
+    pl.semaphore_wait(barrier, guests)
+    start(halo_d[:2] + halo_g[:2] + halo_g1 + halo_d[2:4] + halo_g[2:4] + halo_d[4:] + halo_g[4:])
 
     def inverse(i, span):
         g = rows(G, i, span)
         put(DD, i, span, jnp.where(g > 0.0, 1.0 / jnp.where(g > 0.0, g, 1.0), 0.0))
 
-    def fine_pre(i):
-        c = rows(D, i, FINE)
-        n = rows(G, i, FINE) * coupled(D, i, FINE, c, 1.0)
-        put(FP, i, FINE, ALPHA * c + BETA * n)
-
-    def fine_rest(i):
-        c = rows(FP, i, FINE)
-        return rows(DD, i, FINE) * (MID * rows(D, i, FINE) - c) + coupled(FP, i, FINE, c, 1.0)
-
-    def target_one(k):
+    def within(i):
+        return tuple(step for step in (-1, 1) if 4 <= i + step <= 11)
+
+    def fine_pre(i, span, planes):
+        c = rows(D, i, span)
+        n = rows(G, i, span) * coupled(D, i, span, c, 1.0, planes)
+        put(FP, i, span, ALPHA * c + BETA * n)
+
+    def fine_rest(i, span):
+        c = rows(FP, i, span)
+        return rows(DD, i, span) * (MID * rows(D, i, span) - c) + coupled(FP, i, span, c, 1.0, within(i))
+
+    def target_one(k, span, span1):
         i = 2 * k - 4
-        total = fine_rest(i) + fine_rest(i + 1)
-        put(D1, k, ONE, rows(G1, k, ONE) * packed(total, lax.rem(k, 4), 80) * (1.0 / MID))
-
-    for h in (halo_g, halo_d, halo_g1):
-        wait_recv(h[:2])
-
-    def inverse_y(i):
-        inverse(i, (8, 8))
-        inverse(i, (80, 8))
-
-    loop(4, 12, inverse_y)
-    loop(5, 11, fine_pre)
-    loop(5, 7, target_one)
-    ready = []
-    for n, (dx, to) in enumerate([(1, 1), (-1, 9)]):
-        x, y = at(dx, 0)
-        ready.append((
-            has_x[dx],
-            has_x[-dx],
-            copy(
-                D1.at[pl.ds(5, 2), pl.ds(8, 48)], D1.at[pl.ds(to, 2), pl.ds(8, 48)],
-                s_one.at[n], r_one.at[n], x, y,
-            ),
-        ))
-    start(ready)
-
-    for h in (halo_g, halo_d, halo_g1):
-        wait_recv(h[2:])
-
-    for i in (2, 3, 12, 13):
-        inverse(i, FINE)
-    loop(1, 5, fine_pre)
-    loop(11, 15, fine_pre)
-    loop(3, 5, target_one)
-    loop(7, 9, target_one)
-
-    wait_recv(ready)
+        total = fine_rest(i, span) + fine_rest(i + 1, span)
+        put(D1, k, span1, rows(G1, k, span1) * packed(total, k - 4, span[1]) * (1.0 / MID))
+
+    for i in range(4, 12):
+        fine_pre(i, INNER_PRE, within(i))
+    for k in range(4, 8):
+        target_one(k, INNER, INNER1)
+
+    wait_recv(halo_d[:2] + halo_g[:2] + halo_g1)
+    start(near_g1)
+    for i in range(4, 12):
+        for span, _ in ENDS:
+            inverse(i, (span[0] if span[0] == 8 else 80, 8))
+            fine_pre(i, span, within(i))
+    for k in range(4, 8):
+        for span, span1 in ENDS:
+            target_one(k, span, span1)
+    start(near_d1 + q_g + a_g + more_g1 + more_d1)
+
+    wait_recv(halo_d[2:] + halo_g[2:])
+    wait_send(near_d1)
+    for own, other, near, far in ((4, 3, 4, 3), (11, 12, 7, 8)):
+        inverse(other, FINE)
+        fine_pre(other, FINE, (-1, 1))
+        put(DL, own, FINE, BETA * rows(G, own, FINE) * rows(D, other, FINE))
+        put(DL, other, FINE, BETA * rows(G, other, FINE) * rows(D, own, FINE))
+        put(FP, own, FINE, rows(FP, own, FINE) + rows(DL, own, FINE))
+
+    def lack(i, beyond):
+        c = rows(DL, i, FINE)
+        return c + rows(FP, beyond, FINE) + coupled(DL, i, FINE, c, 1.0, ()) - rows(DD, i, FINE) * c
+
+    for own, other, near in ((4, 3, 4), (11, 12, 7)):
+        more = packed(lack(own, other), near - 4, 80)
+        put(D1, near, ONE, rows(D1, near, ONE) + rows(G1, near, ONE) * more * (1.0 / MID))
+    wait_recv(near_g1 + near_d1)
+    for own, other, far in ((4, 3, 3), (11, 12, 8)):
+        more = packed(lack(other, own), 1 if far == 3 else 2, 80)
+        put(D1, far, ONE, rows(D1, far, ONE) + rows(G1, far, ONE) * more * (1.0 / MID))
 
     def one_pre(i):
         c = rows(D1, i, ONE)
@@ -385,22 +417,12 @@
     both = [(b + swap(b)) * (0.25 / MID2) for b in both]
     put(QD, 0, OWN1, rows(QG, 0, OWN1) * first(both[0], both[0], both[1]))
     start(q_d + a_d)
-    moved = []
-    for n, (dx, frm, to) in enumerate([(1, 4, 0), (-1, 6, 10)]):
-        x, y = at(dx, 0)
-        moved.append((
-            has_x[dx],
-            has_x[-dx],
-            copy(
-                OP.at[pl.ds(frm, 2), pl.ds(8, 48)], OP.at[pl.ds(to, 2), pl.ds(8, 48)],
-                s_op.at[n], r_op.at[n], x, y,
-            ),
-        ))
-    start(moved)
+    start(more_op + more_g + more_fp)
+    wait_recv(more_g1 + more_d1)
     one_pre(2)
     one_pre(9)
 
-    wait_send(halo_g + halo_d + halo_g1 + q_g + a_g + ready)
+    wait_send(halo_g + halo_d + halo_g1 + near_g1 + q_g + a_g + more_g1 + more_d1)
     wait_recv(q_g)
 
     @pl.when(far_block)
@@ -481,7 +503,7 @@
     def _():
         clear(CE, (4, 5), TWO)
 
-    wait_recv(moved)
+    wait_recv(more_op + more_g + more_fp)
 
     def one_start(k):
         for i in (2 * k, 2 * k + 1):
@@ -541,7 +563,7 @@
     for k in range(4):
         returned(res_out, k, rest(4 + 2 * k), rest(5 + 2 * k))
 
-    wait_send(q_d + a_d + moved)
+    wait_send(q_d + a_d + more_op + more_g + more_fp)
 
 
 def cycle(forcing, helmholtz):
@@ -566,7 +588,7 @@
             two, buf(10, 64), buf(10, 64), buf(10, 64), two, buf(4, 64), buf(4, 64), buf(4, 64), buf(4, 64),
             buf(4, 128), buf(4, 80),
             buf(512), buf(512), dma((2,)),
-            dma((3, 8)), dma((3, 8)), dma((2,)), dma((2,)), dma((2,)), dma((2,)),
+            dma((3, 8)), dma((3, 8)), dma((7, 2)), dma((7, 2)),
             dma((2, 4, 3)), dma((2, 4, 3)), dma((2, 2, 3)), dma((2, 4, 3)),
         ],
         compiler_params=pltpu.CompilerParams(

time: 32.6 us -> 29.8 us (0.914)
  the two profiles are of different devices: /device:TPU:217 before, /device:TPU:207 now
where the time goes in v4:
time: 29.8 us; the launch traced here: 29.7 us
  Pallas kernels  27.6 us (93%)
  local copies, waits for them, and re-layouts  1.41 us (5%)
  between operations  0.64 us (2%)
    pallas_call x1, Pallas kernels, cycle(): pl.pallas_call(kernel, out_shape=(out, out), in_specs=[pl.BlockSpec(memor...  27.6 us
    unnamed x2, local copies, waits for them, and re-layouts  1.41 us

profile of v4, /device:TPU:207, one launch (start us, length us, event | category | flops | bytes accessed | tf_op | source)
XLA Modules:
  0.0 29.7 jit_solution(14125003197256497560)
XLA Ops:
  0.6 27.6 %vcycle.1 = (f32[512,128]{1,0:T(8,128)S(1)}, f32[512,128]{1,0:T(8,128)S(1)}) custom-call(f32[512,128]{1,0:T(8,128)} %bitcast.6, f32[512,128]{1,0:T(8,128)} %bitcast.7), custom_call_target="tpu_custom_call" | custom-call | tf_op jit(solution)/shard_map/vcycle/pallas_call | solution.py:580
  28.3 0.7 %copy.6 = f32[64,8,128]{2,1,0:T(8,128)} copy(f32[64,8,128]{2,1,0:T(8,128)S(1)} %bitcast.5) | data formatting | bytes 524288
  29.0 0.7 %copy.7 = f32[64,8,128]{2,1,0:T(8,128)} copy(f32[64,8,128]{2,1,0:T(8,128)S(1)} %bitcast.4) | data formatting | bytes 524288

commit v5 on v4

--- a/solution.py
+++ b/solution.py
@@ -36,8 +36,50 @@
 ENDS = (((8, 16), (12, 8)), ((72, 16), (44, 8)))
 
 
+def lanes():
+    return lax.broadcasted_iota(jnp.int32, (8, 128), 1)
+
+
+def like(mask, value):
+    return jnp.broadcast_to(mask[0:1], value.shape)
+
+
+def first(value, a, b):
+    return jnp.where(like(lanes() < 64, value), a, b)
+
+
+def swap(value):
+    return pltpu.roll(value, 64, 1)
+
+
+def vertical(c):
+    level = lax.rem(lanes(), 64)
+    below = jnp.where(like(level > 0, c), pltpu.roll(c, 1, 1), 0.0)
+    above = jnp.where(like(level < 63, c), pltpu.roll(c, 127, 1), 0.0)
+    return below + above
+
+
+def rows(ref, i, span, shift=0):
+    return ref[i, pl.ds(span[0] + shift, span[1]), :]
+
+
+def beside(ref, i, span, c, planes):
+    mixed = first(c, rows(ref, i, span, 1), rows(ref, i, span, -1))
+    flat = swap(c + mixed)
+    for step in planes:
+        flat = flat + rows(ref, i + step, span)
+    return flat
+
+
+def coupled(ref, i, span, c, weight, planes=(-1, 1)):
+    flat = beside(ref, i, span, c, planes)
+    if weight != 1.0:
+        flat = weight * flat
+    return 2.0 * vertical(c) + flat
+
+
 def kernel(
-    f_hbm, h_hbm, sol_out, res_out,
+    f_hbm, h_hbm, solved, left,
     S, G, DD, D, FP, V, DL, PE,
     G1, D1, DD1, OP, V1, DL1, CE,
     WG, WA, WB, WR, WV, QG, QD, AG, AD,
@@ -49,38 +91,7 @@
     nx, ny = lax.axis_size("gx"), lax.axis_size("gy")
     group, pos = gx // 4, lax.rem(gx, 4)
 
-    lane = lax.broadcasted_iota(jnp.int32, (8, 128), 1)
-    level = lax.rem(lane, 64)
-
-    def like(mask, value):
-        return jnp.broadcast_to(mask[0:1], value.shape)
-
-    def first(value, a, b):
-        return jnp.where(like(lane < 64, value), a, b)
-
-    def swap(value):
-        return pltpu.roll(value, 64, 1)
-
-    def vertical(c):
-        below = jnp.where(like(level > 0, c), pltpu.roll(c, 1, 1), 0.0)
-        above = jnp.where(like(level < 63, c), pltpu.roll(c, 127, 1), 0.0)
-        return below + above
-
-    def rows(ref, i, span, shift=0):
-        return ref[i, pl.ds(span[0] + shift, span[1]), :]
-
-    def beside(ref, i, span, c, planes):
-        mixed = first(c, rows(ref, i, span, 1), rows(ref, i, span, -1))
-        flat = swap(c + mixed)
-        for step in planes:
-            flat = flat + rows(ref, i + step, span)
-        return flat
-
-    def coupled(ref, i, span, c, weight, planes=(-1, 1)):
-        flat = beside(ref, i, span, c, planes)
-        if weight != 1.0:
-            flat = weight * flat
-        return 2.0 * vertical(c) + flat
+    lane = lanes()
 
     def put(ref, i, span, value):
         ref[i, pl.ds(span[0], span[1]), :] = value
@@ -416,7 +427,7 @@
     both = [one_rest(0) + one_rest(1), one_rest(2) + one_rest(3)]
     both = [(b + swap(b)) * (0.25 / MID2) for b in both]
     put(QD, 0, OWN1, rows(QG, 0, OWN1) * first(both[0], both[0], both[1]))
-    start(q_d + a_d)
+    start(a_d + q_d)
     start(more_op + more_g + more_fp)
     wait_recv(more_g1 + more_d1)
     one_pre(2)
@@ -547,23 +558,31 @@
 
     loop(3, 13, fine_post)
 
-    def returned(ref, k, a, b):
-        TS[k, pl.ds(0, 64, stride=2), :] = first(a, a, swap(b))
-        TS[k, pl.ds(1, 64, stride=2), :] = first(a, swap(a), b)
-        both = TS[k].T
-        ref[pl.ds(2 * k, 64, stride=8), :] = both[:64]
-        ref[pl.ds(2 * k + 1, 64, stride=8), :] = both[64:]
-
-    def rest(i):
+    for i in range(4, 12):
         c = rows(S, i, OWN)
-        return rows(DD, i, OWN) * (MID * rows(D, i, OWN) - c) + coupled(S, i, OWN, c, 1.0)
-
-    for k in range(4):
-        returned(sol_out, k, rows(S, 4 + 2 * k, OWN), rows(S, 5 + 2 * k, OWN))
-    for k in range(4):
-        returned(res_out, k, rest(4 + 2 * k), rest(5 + 2 * k))
+        solved[i - 4] = c
+        left[i - 4] = rows(DD, i, OWN) * (MID * rows(D, i, OWN) - c) + coupled(S, i, OWN, c, 1.0)
 
     wait_send(q_d + a_d + more_op + more_g + more_fp)
+
+
+def give_back(solved, left, solved_hbm, left_hbm, a_out, b_out, TS, sems):
+    copies = []
+    for which, (source, target, hbm) in enumerate(
+        ((solved, a_out, solved_hbm), (left, b_out, left_hbm))
+    ):
+        for k in range(4):
+            a, b = source[2 * k], source[2 * k + 1]
+            TS[which, k, pl.ds(0, 64, stride=2), :] = first(a, a, swap(b))
+            TS[which, k, pl.ds(1, 64, stride=2), :] = first(a, swap(a), b)
+            both = TS[which, k].T
+            target[pl.ds(2 * k, 64, stride=8), :] = both[:64]
+            target[pl.ds(2 * k + 1, 64, stride=8), :] = both[64:]
+        out = pltpu.make_async_copy(target, hbm, sems.at[which])
+        out.start()
+        copies.append(out)
+    for out in copies:
+        out.wait()
 
 
 def cycle(forcing, helmholtz):
@@ -577,9 +596,10 @@
     dma = pltpu.SemaphoreType.DMA
     out = jax.ShapeDtypeStruct(flat, jnp.float32)
     vmem = pl.BlockSpec(memory_space=pltpu.VMEM)
-    solved, rest = pl.pallas_call(
+    turned = jax.ShapeDtypeStruct((8, 64, 128), jnp.float32)
+    passed = pl.pallas_call(
         kernel,
-        out_shape=(out, out),
+        out_shape=(turned, turned),
         in_specs=[pl.BlockSpec(memory_space=pl.ANY)] * 2,
         out_specs=(vmem, vmem),
         scratch_shapes=[
@@ -596,6 +616,16 @@
         ),
         name="vcycle",
     )(forcing.reshape(flat), helmholtz.reshape(flat))
+    anywhere = pl.BlockSpec(memory_space=pl.ANY)
+    solved, rest = pl.pallas_call(
+        give_back,
+        out_shape=(out, out),
+        in_specs=[vmem] * 2,
+        out_specs=(anywhere, anywhere),
+        scratch_shapes=[buf(512), buf(512), buf(2, 4, 128), dma((2,))],
+        compiler_params=pltpu.CompilerParams(vmem_limit_bytes=8 * 2**20),
+        name="give_back",
+    )(*passed)
     return solved.reshape(shape), rest.reshape(shape)
 
 

time: 29.8 us -> 28.9 us (0.970)
  the two profiles are of different devices: /device:TPU:207 before, /device:TPU:215 now
where the time goes in v5:
time: 28.9 us; the launch traced here: 28.8 us
  Pallas kernels  28.1 us (97%)
  between operations  0.64 us (2%)
    pallas_call x1, Pallas kernels, cycle(): pl.pallas_call(kernel, out_shape=(turned, turned), in_specs=[pl.BlockSpec...  27 us
    pallas_call x1, Pallas kernels, cycle(): pl.pallas_call(give_back, out_shape=(out, out), in_specs=[vmem] * 2, out_...  1.1 us

profile of v5, /device:TPU:215, one launch (start us, length us, event | category | flops | bytes accessed | tf_op | source)
XLA Modules:
  0.0 28.8 jit_solution(14680365279737803909)
XLA Ops:
  0.6 27.0 %vcycle.1 = (f32[8,64,128]{2,1,0:T(8,128)S(1)}, f32[8,64,128]{2,1,0:T(8,128)S(1)}) custom-call(f32[512,128]{1,0:T(8,128)} %bitcast.4, f32[512,128]{1,0:T(8,128)} %bitcast.5), custom_call_target="tpu_custom_call" | custom-call | tf_op jit(solution)/shard_map/vcycle/pallas_call | solution.py:600
  27.7 1.1 %give_back.1 = (f32[512,128]{1,0:T(8,128)}, f32[512,128]{1,0:T(8,128)}) custom-call(f32[8,64,128]{2,1,0:T(8,128)S(1)} %get-tuple-element.6.solved, f32[8,64,128]{2,1,0:T(8,128)S(1)} %get-tuple-element.7.left), custom_call_target="tpu_custom_call" | custom-call | tf_op jit(solution)/shard_map/give_back/pallas_call | solution.py:620

commit v6 on v5

--- a/solution.py
+++ b/solution.py
@@ -138,23 +138,33 @@
     def greet(x, y):
         pl.semaphore_signal(barrier, inc=1, device_id=(x, y), device_id_type=MESH)
 
-    def greet_column(dy):
-        for k in range(4):
-            if (k, dy) != (0, 0):
-                greet(mates[k], ys[dy])
-
-        @pl.when((pos == 0) & has_group[-1])
-        def _():
-            for k in range(4):
-                greet(lax.rem(4 * group + nx - 4 + k, nx), ys[dy])
-
-        @pl.when((pos == 3) & has_group[1])
-        def _():
-            for k in range(4):
-                greet(lax.rem(4 * group + 4 + k, nx), ys[dy])
-
-    for dy in range(3):
-        when(has_y[sides[dy]], functools.partial(greet_column, dy))
+    def greet_columns(targets):
+        for dy in (0, 1, 2):
+            def act(dy=dy):
+                for x in targets:
+                    greet(x, ys[dy])
+
+            when(has_y[sides[dy]], act)
+
+    @pl.when((pos == 0) & has_group[-1])
+    def _():
+        greet_columns([lax.rem(4 * group + nx - 1, nx)])
+
+    @pl.when((pos == 3) & has_group[1])
+    def _():
+        greet_columns([lax.rem(4 * group + 4, nx)])
+
+    for dy in (1, 2):
+        when(has_y[sides[dy]], functools.partial(greet, gx, ys[dy]))
+    greet_columns(mates[1:])
+
+    @pl.when((pos == 0) & has_group[-1])
+    def _():
+        greet_columns([lax.rem(4 * group + nx - 4 + k, nx) for k in range(3)])
+
+    @pl.when((pos == 3) & has_group[1])
+    def _():
+        greet_columns([lax.rem(4 * group + 5 + k, nx) for k in range(3)])
 
     columns = one + jnp.where(gy > 0, one, none) + jnp.where(gy < ny - 1, one, none)
     blocks = 4 + jnp.where(has_group[1], one, none) + jnp.where(has_group[-1], one, none)
@@ -353,7 +363,7 @@
         put(D, 4 + 2 * k, OWN, rows(G, 4 + 2 * k, OWN) * f_a * (1.0 / MID))
         put(D, 5 + 2 * k, OWN, rows(G, 5 + 2 * k, OWN) * f_b * (1.0 / MID))
     pl.semaphore_wait(barrier, guests)
-    start(halo_d[:2] + halo_g[:2] + halo_g1 + halo_d[2:4] + halo_g[2:4] + halo_d[4:] + halo_g[4:])
+    start(halo_d[:2] + halo_g[:2] + halo_g1 + halo_d[2:4] + halo_g[2:4] + halo_d[4:] + halo_g[4:] + a_g + q_g + more_g)
 
     def inverse(i, span):
         g = rows(G, i, span)
@@ -390,7 +400,7 @@
     for k in range(4, 8):
         for span, span1 in ENDS:
             target_one(k, span, span1)
-    start(near_d1 + q_g + a_g + more_g1 + more_d1)
+    start(near_d1 + more_g1 + more_d1)
 
     wait_recv(halo_d[2:] + halo_g[2:])
     wait_send(near_d1)
@@ -408,10 +418,9 @@
     for own, other, near in ((4, 3, 4), (11, 12, 7)):
         more = packed(lack(own, other), near - 4, 80)
         put(D1, near, ONE, rows(D1, near, ONE) + rows(G1, near, ONE) * more * (1.0 / MID))
-    wait_recv(near_g1 + near_d1)
-    for own, other, far in ((4, 3, 3), (11, 12, 8)):
-        more = packed(lack(other, own), 1 if far == 3 else 2, 80)
-        put(D1, far, ONE, rows(D1, far, ONE) + rows(G1, far, ONE) * more * (1.0 / MID))
+    wait_recv(near_g1)
+    for own, other, far, slot in ((4, 3, 3, 1), (11, 12, 8, 2)):
+        put(DL1, far, ONE, rows(G1, far, ONE) * packed(lack(other, own), slot, 80) * (1.0 / MID))
 
     def one_pre(i):
         c = rows(D1, i, ONE)
@@ -423,17 +432,23 @@
         c = rows(OP, i, OWN1)
         return DD1[k] * (MID * rows(D1, i, OWN1) - c) + coupled(OP, i, OWN1, c, 0.25)
 
-    loop(3, 9, one_pre)
+    one_pre(5)
+    one_pre(6)
+    wait_recv(near_d1)
+    for far in (3, 8):
+        put(D1, far, ONE, rows(D1, far, ONE) + rows(DL1, far, ONE))
+    for i in (3, 4, 7, 8):
+        one_pre(i)
     both = [one_rest(0) + one_rest(1), one_rest(2) + one_rest(3)]
     both = [(b + swap(b)) * (0.25 / MID2) for b in both]
     put(QD, 0, OWN1, rows(QG, 0, OWN1) * first(both[0], both[0], both[1]))
     start(a_d + q_d)
-    start(more_op + more_g + more_fp)
+    start(more_op + more_fp)
     wait_recv(more_g1 + more_d1)
     one_pre(2)
     one_pre(9)
 
-    wait_send(halo_g + halo_d + halo_g1 + near_g1 + q_g + a_g + more_g1 + more_d1)
+    wait_send(halo_g + halo_d + halo_g1 + near_g1 + q_g + a_g + more_g1 + more_d1 + more_g)
     wait_recv(q_g)
 
     @pl.when(far_block)
@@ -462,6 +477,7 @@
     WR[8, pl.ds(8, 48), :] = keep_up
     WR[9, pl.ds(8, 48), :] = keep_down
 
+    wait_send(q_d + a_d + more_op + more_fp)
     wait_recv(q_d)
 
     @pl.when(far_block)
@@ -562,8 +578,6 @@
         c = rows(S, i, OWN)
         solved[i - 4] = c
         left[i - 4] = rows(DD, i, OWN) * (MID * rows(D, i, OWN) - c) + coupled(S, i, OWN, c, 1.0)
-
-    wait_send(q_d + a_d + more_op + more_g + more_fp)
 
 
 def give_back(solved, left, solved_hbm, left_hbm, a_out, b_out, TS, sems):

time: 28.9 us -> 28.7 us (level)
  the two profiles are of different devices: /device:TPU:215 before, /device:TPU:209 now
where the time goes in v6:
time: 28.7 us; the launch traced here: 28.6 us
  Pallas kernels  27.9 us (97%)
  between operations  0.64 us (2%)
    pallas_call x1, Pallas kernels, cycle(): pl.pallas_call(kernel, out_shape=(turned, turned), in_specs=[pl.BlockSpec...  26.8 us
    pallas_call x1, Pallas kernels, cycle(): pl.pallas_call(give_back, out_shape=(out, out), in_specs=[vmem] * 2, out_...  1.1 us

profile of v6, /device:TPU:209, one launch (start us, length us, event | category | flops | bytes accessed | tf_op | source)
XLA Modules:
  0.0 28.6 jit_solution(7095357531615878235)
XLA Ops:
  0.6 26.8 %vcycle.1 = (f32[8,64,128]{2,1,0:T(8,128)S(1)}, f32[8,64,128]{2,1,0:T(8,128)S(1)}) custom-call(f32[512,128]{1,0:T(8,128)} %bitcast.4, f32[512,128]{1,0:T(8,128)} %bitcast.5), custom_call_target="tpu_custom_call" | custom-call | tf_op jit(solution)/shard_map/vcycle/pallas_call | solution.py:614
  27.5 1.1 %give_back.1 = (f32[512,128]{1,0:T(8,128)}, f32[512,128]{1,0:T(8,128)}) custom-call(f32[8,64,128]{2,1,0:T(8,128)S(1)} %get-tuple-element.6.solved, f32[8,64,128]{2,1,0:T(8,128)S(1)} %get-tuple-element.7.left), custom_call_target="tpu_custom_call" | custom-call | tf_op jit(solution)/shard_map/give_back/pallas_call | solution.py:634

commit v7 on v6

--- a/solution.py
+++ b/solution.py
@@ -400,7 +400,7 @@
     for k in range(4, 8):
         for span, span1 in ENDS:
             target_one(k, span, span1)
-    start(near_d1 + more_g1 + more_d1)
+    start(near_d1 + more_g1 + more_d1 + more_fp)
 
     wait_recv(halo_d[2:] + halo_g[2:])
     wait_send(near_d1)
@@ -443,7 +443,7 @@
     both = [(b + swap(b)) * (0.25 / MID2) for b in both]
     put(QD, 0, OWN1, rows(QG, 0, OWN1) * first(both[0], both[0], both[1]))
     start(a_d + q_d)
-    start(more_op + more_fp)
+    start(more_op)
     wait_recv(more_g1 + more_d1)
     one_pre(2)
     one_pre(9)
@@ -463,7 +463,7 @@
             write(2 * s + 1, first(own, swap(own), far))
 
     def write_g(i, value):
-        put(WG, i, TWO, value)
+        put(WG, i, TWO, 2.0 * value)
 
     assemble(QG, AG, write_g)
     clear(WA, (0, 9), TWO)
@@ -474,10 +474,16 @@
     cut_high = (lax.rem(gy, 4) == 3).astype(jnp.float32)
     keep_up = 1.0 - jnp.where(at_row == 8, cut_low, 0.0) - jnp.where(at_row == 40, cut_high, 0.0)
     keep_down = 1.0 - jnp.where(at_row == 7, cut_low, 0.0) - jnp.where(at_row == 39, cut_high, 0.0)
-    WR[8, pl.ds(8, 48), :] = keep_up
-    WR[9, pl.ds(8, 48), :] = keep_down
 
     wait_send(q_d + a_d + more_op + more_fp)
+    wait_recv(more_fp)
+    for i in range(2, 14):
+        put(V, i, POST, coupled(FP, i, POST, rows(FP, i, POST), 1.0))
+
+    def one_coupled(i):
+        put(V1, i, ONE, coupled(OP, i, ONE, rows(OP, i, ONE), 0.25))
+
+    loop(3, 9, one_coupled)
     wait_recv(q_d)
 
     @pl.when(far_block)
@@ -502,9 +508,11 @@
         def relax(x, now=now, later=later, keep=keep, gain=gain, final=final):
             c = rows(now, x + 1, TWO)
             flat = rows(now, x, TWO) + rows(now, x + 2, TWO)
-            flat = flat + rows(WR, 8, TWO) * rows(now, x + 1, TWO, -1)
-            flat = flat + rows(WR, 9, TWO) * rows(now, x + 1, TWO, 1)
-            n = rows(WG, x, TWO) * (2.0 * vertical(c) + 0.0625 * flat)
+            up, down = rows(now, x + 1, TWO, -1), rows(now, x + 1, TWO, 1)
+            up = jnp.concatenate([up[:16] * keep_up[:16], up[16:32], up[32:] * keep_up[32:]], axis=0)
+            down = jnp.concatenate([down[:16] * keep_down[:16], down[16:32], down[32:] * keep_down[32:]], axis=0)
+            flat = flat + up + down
+            n = rows(WG, x, TWO) * (vertical(c) + 0.03125 * flat)
             rest = rows(WR, x, TWO) - c + n
             d = keep * c + gain * rest
             if not final:
@@ -530,27 +538,28 @@
     def _():
         clear(CE, (4, 5), TWO)
 
-    wait_recv(more_op + more_g + more_fp)
+    wait_recv(more_op + more_g)
+
+    for i in (1, 2, 9, 10):
+        one_coupled(i)
 
     def one_start(k):
-        for i in (2 * k, 2 * k + 1):
-            put(V1, i, ONE, rows(OP, i, ONE) + rows(CE, k, ONE))
-
-    def change(v, g, d0, to, span, weight):
-        def body(i):
-            c = rows(v, i, span)
-            n = rows(g, i, span) * coupled(v, i, span, c, weight)
-            put(to, i, span, rows(d0, i, span) + (n - c) * (1.0 / MID))
-
-        return body
+        e = rows(CE, k, ONE)
+        shared = 2.0 * vertical(e) + 0.25 * (first(e, rows(CE, k, ONE, -1), rows(CE, k, ONE, 1)) + 2.0 * e)
+        for i, beyond in ((2 * k, k - 1), (2 * k + 1, k + 1)):
+            if 1 <= i <= 10:
+                v = rows(OP, i, ONE) + e
+                n = rows(G1, i, ONE) * (rows(V1, i, ONE) + shared + 0.25 * rows(CE, beyond, ONE))
+                put(DL1, i, ONE, rows(D1, i, ONE) + (n - v) * (1.0 / MID))
+                put(V1, i, ONE, v)
 
     def smoothed(v, g, d, i, span, weight):
         c = rows(d, i, span)
         n = rows(g, i, span) * coupled(d, i, span, c, weight)
         return rows(v, i, span) + ALPHA * c + BETA * n
 
-    loop(0, 6, one_start)
-    loop(1, 11, change(V1, G1, D1, DL1, ONE, 0.25))
+    for k in range(6):
+        one_start(k)
 
     def one_post(i):
         value = smoothed(V1, G1, DL1, i, ONE, 0.25)
@@ -561,13 +570,16 @@
     loop(2, 10, one_post)
 
     def fine_start(k):
-        for i in (2 * k, 2 * k + 1):
-            put(V, i, POST, rows(FP, i, POST) + rows(PE, k, POST))
-
-    put(V, 1, POST, rows(FP, 1, POST) + rows(PE, 0, POST))
-    loop(1, 7, fine_start)
-    put(V, 14, POST, rows(FP, 14, POST) + rows(PE, 7, POST))
-    loop(2, 14, change(V, G, D, DL, POST, 1.0))
+        e = rows(PE, k, POST)
+        shared = 2.0 * vertical(e) + first(e, rows(PE, k, POST, -1), rows(PE, k, POST, 1)) + 2.0 * e
+        for i, beyond in ((2 * k, k - 1), (2 * k + 1, k + 1)):
+            v = rows(FP, i, POST) + e
+            n = rows(G, i, POST) * (rows(V, i, POST) + shared + rows(PE, beyond, POST))
+            put(DL, i, POST, rows(D, i, POST) + (n - v) * (1.0 / MID))
+            put(V, i, POST, v)
+
+    for k in range(1, 7):
+        fine_start(k)
 
     def fine_post(i):
         put(S, i, POST, smoothed(V, G, DL, i, POST, 1.0))

time: 28.7 us -> 28.3 us (0.986)
  the two profiles are of different devices: /device:TPU:209 before, /device:TPU:1 now
where the time goes in v7:
time: 28.3 us; the launch traced here: 28.1 us
  Pallas kernels  27.5 us (97%)
  between operations  0.64 us (2%)
    pallas_call x1, Pallas kernels, cycle(): pl.pallas_call(kernel, out_shape=(turned, turned), in_specs=[pl.BlockSpec...  26.4 us
    pallas_call x1, Pallas kernels, cycle(): pl.pallas_call(give_back, out_shape=(out, out), in_specs=[vmem] * 2, out_...  1.1 us

profile of v7, /device:TPU:1, one launch (start us, length us, event | category | flops | bytes accessed | tf_op | source)
XLA Modules:
  0.0 28.1 jit_solution(10316035541138421826)
XLA Ops:
  0.6 26.4 %vcycle.1 = (f32[8,64,128]{2,1,0:T(8,128)S(1)}, f32[8,64,128]{2,1,0:T(8,128)S(1)}) custom-call(f32[512,128]{1,0:T(8,128)} %bitcast.4, f32[512,128]{1,0:T(8,128)} %bitcast.5), custom_call_target="tpu_custom_call" | custom-call | tf_op jit(solution)/shard_map/vcycle/pallas_call | solution.py:626
  27.0 1.1 %give_back.1 = (f32[512,128]{1,0:T(8,128)}, f32[512,128]{1,0:T(8,128)}) custom-call(f32[8,64,128]{2,1,0:T(8,128)S(1)} %get-tuple-element.6.solved, f32[8,64,128]{2,1,0:T(8,128)S(1)} %get-tuple-element.7.left), custom_call_target="tpu_custom_call" | custom-call | tf_op jit(solution)/shard_map/give_back/pallas_call | solution.py:646

commit v8 on v7

--- a/solution.py
+++ b/solution.py
@@ -103,8 +103,8 @@
 
         lax.fori_loop(lo, hi, step, 0, unroll=min(unroll, hi - lo))
 
-    load_h = pltpu.make_async_copy(h_hbm, h_in, s_in.at[0])
-    load_f = pltpu.make_async_copy(f_hbm, f_in, s_in.at[1])
+    load_h = pltpu.make_async_copy(h_hbm, h_in.at[pl.ds(0, 512)], s_in.at[0])
+    load_f = pltpu.make_async_copy(f_hbm, f_in.at[pl.ds(0, 512)], s_in.at[1])
     load_h.start()
     load_f.start()
 
@@ -327,7 +327,7 @@
         both = jnp.concatenate(
             [ref[pl.ds(2 * k, 64, stride=8), :], ref[pl.ds(2 * k + 1, 64, stride=8), :]], axis=0
         )
-        TS[k] = both.T
+        TS[k, pl.ds(0, 128), :] = both.T
         even = TS[k, pl.ds(0, 64, stride=2), :]
         odd = TS[k, pl.ds(1, 64, stride=2), :]
         return first(even, even, swap(odd)), first(even, swap(even), odd)
@@ -601,10 +601,10 @@
             a, b = source[2 * k], source[2 * k + 1]
             TS[which, k, pl.ds(0, 64, stride=2), :] = first(a, a, swap(b))
             TS[which, k, pl.ds(1, 64, stride=2), :] = first(a, swap(a), b)
-            both = TS[which, k].T
+            both = TS[which, k, pl.ds(0, 128), :].T
             target[pl.ds(2 * k, 64, stride=8), :] = both[:64]
             target[pl.ds(2 * k + 1, 64, stride=8), :] = both[64:]
-        out = pltpu.make_async_copy(target, hbm, sems.at[which])
+        out = pltpu.make_async_copy(target.at[pl.ds(0, 512)], hbm, sems.at[which])
         out.start()
         copies.append(out)
     for out in copies:
@@ -632,8 +632,8 @@
             fine, fine, fine, fine, fine, fine, fine, buf(8, 96),
             one, one, buf(4, 32), one, one, one, buf(6, 64),
             two, buf(10, 64), buf(10, 64), buf(10, 64), two, buf(4, 64), buf(4, 64), buf(4, 64), buf(4, 64),
-            buf(4, 128), buf(4, 80),
-            buf(512), buf(512), dma((2,)),
+            buf(4, 144), buf(4, 96),
+            buf(576), buf(576), dma((2,)),
             dma((3, 8)), dma((3, 8)), dma((7, 2)), dma((7, 2)),
             dma((2, 4, 3)), dma((2, 4, 3)), dma((2, 2, 3)), dma((2, 4, 3)),
         ],
@@ -648,7 +648,7 @@
         out_shape=(out, out),
         in_specs=[vmem] * 2,
         out_specs=(anywhere, anywhere),
-        scratch_shapes=[buf(512), buf(512), buf(2, 4, 128), dma((2,))],
+        scratch_shapes=[buf(576), buf(576), buf(2, 4, 144), dma((2,))],
         compiler_params=pltpu.CompilerParams(vmem_limit_bytes=8 * 2**20),
         name="give_back",
     )(*passed)

time: 28.3 us -> 28.3 us (level)
  no operation moved by 1% of the time
where the time goes in v8:
time: 28.3 us; the launch traced here: 28.1 us
  Pallas kernels  27.5 us (97%)
  between operations  0.64 us (2%)
    pallas_call x1, Pallas kernels, cycle(): pl.pallas_call(kernel, out_shape=(turned, turned), in_specs=[pl.BlockSpec...  26.4 us
    pallas_call x1, Pallas kernels, cycle(): pl.pallas_call(give_back, out_shape=(out, out), in_specs=[vmem] * 2, out_...  1.1 us

profile of v8, /device:TPU:1, one launch (start us, length us, event | category | flops | bytes accessed | tf_op | source)
XLA Modules:
  0.0 28.1 jit_solution(5058322942188505201)
XLA Ops:
  0.6 26.4 %vcycle.1 = (f32[8,64,128]{2,1,0:T(8,128)S(1)}, f32[8,64,128]{2,1,0:T(8,128)S(1)}) custom-call(f32[512,128]{1,0:T(8,128)} %bitcast.4, f32[512,128]{1,0:T(8,128)} %bitcast.5), custom_call_target="tpu_custom_call" | custom-call | tf_op jit(solution)/shard_map/vcycle/pallas_call | solution.py:626
  27.0 1.1 %give_back.1 = (f32[512,128]{1,0:T(8,128)}, f32[512,128]{1,0:T(8,128)}) custom-call(f32[8,64,128]{2,1,0:T(8,128)S(1)} %get-tuple-element.6.solved, f32[8,64,128]{2,1,0:T(8,128)S(1)} %get-tuple-element.7.left), custom_call_target="tpu_custom_call" | custom-call | tf_op jit(solution)/shard_map/give_back/pallas_call | solution.py:646
